TPU v7x, 32 devices: a whole 2x2x4 slice. The times are simulated.
32 devices in a mesh: dp: 2 (over core), expert: 8 (over z, x), replica: 2 (over y).
Axes of the slice: x: 2, y: 2, z: 4, core: 2. Of those that a mesh axis runs over, the one named last changes fastest.
Arguments:
- tokens: bfloat16 [4096, 4096], P(('dp', 'expert', 'replica')), may hold values from -6 to 6
- expert_ids: int32 [4096, 8], P(('dp', 'expert', 'replica')), may hold values from 0 to 15, all different within a row; in each aligned block of 128 rows (0 to 127, 128 to 255, ...) at most 96 rows name the same one
- router_weight: bfloat16 [4096, 16], replicated, may hold values from -0.09375 to 0.09375
- gate_weight: bfloat16 [16, 4096, 768], P(('expert', 'replica')), may hold values from -0.09375 to 0.09375
- up_weight: bfloat16 [16, 4096, 768], P(('expert', 'replica')), may hold values from -0.09375 to 0.09375
- down_weight: bfloat16 [16, 768, 4096], P(('expert', 'replica')), may hold values from -0.21875 to 0.21875
- cotangent: bfloat16 [4096, 4096], P(('dp', 'expert', 'replica')), may hold values from -0.09375 to 0.09375
Outputs:
- mixed: bfloat16 [4096, 4096], P(('dp', 'expert', 'replica'))
- router_grad: float32 [4096, 16], replicated
Inputs may be any that keep to these rules, and one draw needn't show every extreme that they name: `expert_ids`: in each aligned block of 128 rows (the rows of one device) no expert is named by more than 96 rows, and in every draw some expert is named by exactly 96 rows of some block.
All inputs are finite; a program needn't handle non-finite values.
Results may differ from a plain program's by a relative error of at most 0.0057.
Values may be sent and summed in bfloat16 or wider, within the bound.
A program may use at most 128 MiB of HBM per device.

v0:
```python
import jax
import jax.numpy as jnp
from jax import lax
from jax.sharding import PartitionSpec as P


def expert_apply(incoming, gate_mat, up_mat, down_mat):
    model_width = incoming.shape[-1]
    flat_rows = incoming.reshape(-1, model_width)
    gate_act = jnp.dot(flat_rows, gate_mat, preferred_element_type=jnp.float32)
    up_act = jnp.dot(flat_rows, up_mat, preferred_element_type=jnp.float32)
    hidden = (jax.nn.silu(gate_act) * up_act).astype(jnp.bfloat16)
    result = jnp.dot(hidden, down_mat, preferred_element_type=jnp.float32).astype(jnp.bfloat16)
    return result.reshape(incoming.shape)


def local(tokens, expert_ids, router_weight, gate_weight, up_weight, down_weight, cotangent):
    tok_rows, model_width = tokens.shape
    top_count = expert_ids.shape[1]
    experts = router_weight.shape[1]
    capacity = 3 * tok_rows * top_count // (2 * experts)
    logits = jnp.dot(tokens, router_weight, preferred_element_type=jnp.float32)
    onehot = (expert_ids[:, :, None] == jnp.arange(experts, dtype=jnp.int32)[None, None, :]).astype(
        jnp.float32
    )
    chosen = jnp.einsum("tke,te->tk", onehot, logits, precision=lax.Precision.HIGHEST)
    raised = jnp.exp(chosen)
    gate_probs = raised / jnp.sum(raised, axis=1, keepdims=True)
    flat_ids = expert_ids.reshape(-1)
    member = (flat_ids[:, None] == jnp.arange(experts, dtype=jnp.int32)[None, :]).astype(jnp.int32)
    before = jnp.cumsum(member, axis=0) - member
    slot_place = jnp.sum(before * member, axis=1)
    target = flat_ids * capacity + slot_place
    token_of_slot = jnp.arange(tok_rows * top_count, dtype=jnp.int32) // top_count
    outbox = (
        jnp.zeros((experts * capacity, model_width), jnp.bfloat16)
        .at[target]
        .set(tokens[token_of_slot])
    )
    outbox = outbox.reshape(experts, capacity, model_width)
    gate_mat = gate_weight[0]
    up_mat = up_weight[0]
    down_mat = down_weight[0]
    returned = lax.all_to_all(
        expert_apply(
            lax.all_to_all(outbox, ("expert", "replica"), split_axis=0, concat_axis=0, tiled=True),
            gate_mat,
            up_mat,
            down_mat,
        ),
        ("expert", "replica"),
        split_axis=0,
        concat_axis=0,
        tiled=True,
    )
    returned = returned.reshape(experts * capacity, model_width)
    slot_rows = returned[target].reshape(tok_rows, top_count, model_width)
    mixed = jnp.sum(gate_probs[:, :, None] * slot_rows, axis=1).astype(jnp.bfloat16)
    slot_dots = jnp.einsum("tkd,td->tk", slot_rows, cotangent, preferred_element_type=jnp.float32)
    logit_grad = gate_probs * (slot_dots - jnp.sum(gate_probs * slot_dots, axis=1, keepdims=True))
    grad_table = jnp.einsum("tk,tke->te", logit_grad, onehot, precision=lax.Precision.HIGHEST)
    local_grad = jnp.dot(tokens.astype(jnp.float32).T, grad_table, precision=lax.Precision.HIGHEST)
    router_grad = lax.psum(local_grad, ("dp", "expert", "replica"))
    return (mixed, router_grad)


def solution(mesh):
    in_specs = (
        P(("dp", "expert", "replica"), None),
        P(("dp", "expert", "replica"), None),
        P(),
        P(("expert", "replica"), None, None),
        P(("expert", "replica"), None, None),
        P(("expert", "replica"), None, None),
        P(("dp", "expert", "replica"), None),
    )
    out_specs = (P(("dp", "expert", "replica"), None), P())
    return jax.shard_map(local, mesh=mesh, in_specs=in_specs, out_specs=out_specs, check_vma=False)
```

profile of v0, /device:TPU:12, one launch (start us, length us, event | category | flops | bytes accessed | tf_op | source)
XLA Modules:
  0.0 847.5 jit_solution(7079940948023439052)
XLA Ops:
  7.2 0.9 copy.12
  8.2 0.7 broadcast_multiply_fusion
  9.0 4.5 reduce-window.6
  13.6 0.1 copy.16
  14.2 7.8 gather_fusion
  22.0 20.1 %scatter_custom_fusion = bf16[1536,4096]{1,0:T(8,128)(2,1)} fusion(s32[1024]{0:T(1024)S(1)} %bitcast.77, bf16[1024,4096]{1,0:T(8,128)(2,1)} %gather_fusion, bf16[]{:T(256)} %constant.27.clone.1), kind=kCustom, calls=%fused_computation.12 | custom fusion | bytes 12583424 | tf_op jit(solution)/shard_map/scatter | solution.py:38
  42.1 279.4 %all_to_all.10 = bf16[16,96,4096]{2,1,0:T(8,128)(2,1)S(1)} all-to-all(bf16[16,96,4096]{2,1,0:T(8,128)(2,1)} %bitcast.64), channel_id=1, replica_groups=mesh['dp'=2,'expert'=8,'replica'=2] {'expert','replica'}, dimensions={0} | all-to-all | bytes 25165824 | tf_op jit(solution)/shard_map/all_to_all | solution.py:46
  321.5 13.3 %fusion.3 = f32[1536,768]{1,0:T(8,128)} fusion(bf16[1536,4096]{1,0:T(8,128)(2,1)S(1)} %bitcast.66, bf16[1,4096,768]{2,1,0:T(8,128)(2,1)} %param.11), kind=kOutput, calls=%fused_computation.8 | convolution fusion | flops 9663676416 | bytes 23592960 | tf_op jit(solution)/shard_map/dot_general | solution.py:11
  334.8 12.2 %multiply_convert_fusion = bf16[1536,768]{1,0:T(8,128)(2,1)S(1)} fusion(f32[1536,768]{1,0:T(8,128)} %fusion.3, bf16[1536,4096]{1,0:T(8,128)(2,1)S(1)} %bitcast.67, bf16[1,4096,768]{2,1,0:T(8,128)(2,1)S(1)} %bitcast.81), kind=kOutput, calls=%fused_computation.14 | convolution fusion | flops 9670754304 | bytes 25952256 | tf_op jit(solution)/shard_map/dot_general | solution.py:10
  347.0 15.1 %convolution_convert_fusion = bf16[1536,4096]{1,0:T(8,128)(2,1)} fusion(bf16[1536,768]{1,0:T(8,128)(2,1)S(1)} %multiply_convert_fusion, bf16[1,768,4096]{2,1,0:T(8,128)(2,1)} %param.12), kind=kOutput, calls=%fused_computation.4 | convolution fusion | flops 9669967872 | bytes 21233664 | tf_op jit(solution)/shard_map/dot_general | solution.py:13
  362.1 6.5 all-to-all-start.1
  368.6 12.1 %all-reduce.2.cloned.1.call-start = ((), (), s32[]{:S(2)}) async-start(), calls=%async_computation.2 | async-start | bytes 524288 | tf_op jit(solution)/shard_map/psum | solution.py:63
  380.7 0.4 fusion.20
  381.1 0.6 fusion.13
  381.7 0.1 exponential_reduce_fusion
  381.9 278.4 %all-to-all-done.1 = bf16[16,96,4096]{2,1,0:T(8,128)(2,1)} async-done(((bf16[16,96,4096]{2,1,0:T(8,128)(2,1)}), bf16[16,96,4096]{2,1,0:T(8,128)(2,1)}, u32[]{:S(2)}, u32[]{:S(2)}) %all-to-all-start.1) | async-done | bytes 12582944 | tf_op jit(solution)/shard_map/all_to_all | solution.py:44
  660.3 21.4 %gather_fusion.1 = bf16[1024,4096]{1,0:T(8,128)(2,1)} fusion(bf16[1536,4096]{1,0:T(8,128)(2,1)} %bitcast.15, s32[1024]{0:T(1024)S(1)} %broadcast_clamp_fusion), kind=kCustom, calls=%fused_computation.1 | custom fusion | bytes 16781312 | tf_op jit(solution)/shard_map/gather | solution.py:57
  681.6 8.8 %fusion = f32[128,1,8]{2,1,0:T(1,128)S(1)} fusion(bf16[1024,4096]{1,0:T(8,128)(2,1)} %gather_fusion.1, bf16[128,4096,1]{1,0,2:T(8,128)(2,1)S(1)} %bitcast.82), kind=kOutput, calls=%fused_computation.5 | convolution fusion | flops 8388608 | bytes 9441280 | tf_op jit(solution)/shard_map/tkd,td->tk/dot_general | solution.py:59
  690.5 0.2 multiply_reduce_fusion.1
  690.8 0.6 fusion.12
  691.4 1.3 convolution_bitcast_fusion
  692.7 12.9 %multiply_reduce_fusion = bf16[128,4096]{1,0:T(8,128)(2,1)} fusion(bf16[1024,4096]{1,0:T(8,128)(2,1)} %gather_fusion.1, f32[128,8]{1,0:T(8,128)S(1)} %get-tuple-element.3), kind=kLoop, calls=%fused_computation.3 | loop fusion | flops 12058624 | bytes 9441280 | tf_op jit(solution)/shard_map/reduce_sum | solution.py:58
  705.6 133.2 %all-reduce.2.cloned.1.call-done = f32[4096,16]{0,1:T(8,128)} async-done(((f32[4096,16]{0,1:T(8,128)}), f32[4096,16]{0,1:T(8,128)}) %all-reduce.2.cloned.1.call-update) | async-done | bytes 262160 | tf_op jit(solution)/shard_map/psum | solution.py:63
  838.8 1.7 copy.29
  (28 shorter events, 0.9 us)
Async XLA Ops:
  7.2 7.0 copy-start
  42.1 292.8 %slice-start = ((s8[6291456]{0:T(1024)(128)(4,1)}), s8[4194304]{0:T(1024)(128)(4,1)S(1)}, s32[]{:S(2)}) async-start(s8[6291456]{0:T(1024)(128)(4,1)} %bitcast.80), calls=%async_computation.3 | async-start | bytes 8388608
  321.5 13.3 %slice-start.1 = ((s8[6291456]{0:T(1024)(128)(4,1)}), s8[2097152]{0:T(1024)(128)(4,1)S(1)}, s32[]{:S(2)}) async-start(s8[6291456]{0:T(1024)(128)(4,1)} %bitcast.80), calls=%async_computation.4 | async-start | bytes 4194304
  362.1 18.6 %copy-start.2 = (bf16[4096,16]{0,1:T(8,128)(2,1)S(1)}, bf16[4096,16]{0,1:T(8,128)(2,1)}, u32[]{:S(2)}) copy-start(bf16[4096,16]{0,1:T(8,128)(2,1)} %param.9) | copy-start | bytes 393220
  362.1 298.1 %all-to-all-start.1 = ((bf16[16,96,4096]{2,1,0:T(8,128)(2,1)}), bf16[16,96,4096]{2,1,0:T(8,128)(2,1)}, u32[]{:S(2)}, u32[]{:S(2)}) async-start(bf16[16,96,4096]{2,1,0:T(8,128)(2,1)} %bitcast.65), calls=%async_computation.1 | async-start | bytes 25165824 | tf_op jit(solution)/shard_map/all_to_all | solution.py:44
  368.6 470.2 %all-reduce.2.cloned.1.call-start = ((), (), s32[]{:S(2)}) async-start(), calls=%async_computation.2 | async-start | bytes 524288 | tf_op jit(solution)/shard_map/psum | solution.py:63
  660.3 21.4 %copy-start.1 = (bf16[128,4096]{1,0:T(8,128)(2,1)S(1)}, bf16[128,4096]{1,0:T(8,128)(2,1)}, u32[]{:S(2)}) copy-start(bf16[128,4096]{1,0:T(8,128)(2,1)} %param.13) | copy-start | bytes 3145732
Sparse Core Ops, SparseCore 0:
  692.8 145.9 all-reduce.1
where the time goes:
time: 857 us; the launch traced here: 848 us
  waiting for transfers between devices  412 us (48%)
  blocking collectives  279 us (33%)
  local copies, waits for them, and re-layouts  52.5 us (6%)
  matrix products  52.4 us (6%)
  other arithmetic  18.7 us (2%)
  starting transfers between devices  18.5 us (2%)
  between operations  14.4 us (2%)
    all_to_all x1, blocking collectives, local(): lax.all_to_all(outbox, ('expert', 'replica'), split_axis=0, concat_axis=0...  279 us
    all_to_all x1, waiting for transfers between devices, local(): lax.all_to_all(expert_apply(lax.all_to_all(outbox, ('expert', 'replica'),...  278 us
    psum x1, waiting for transfers between devices, local(): router_grad = lax.psum(local_grad, ('dp', 'expert', 'replica'))  133 us
    gather x1, local copies, waits for them, and re-layouts, local(): slot_rows = returned[target].reshape(tok_rows, top_count, model_width)  21.4 us
    scatter x1, local copies, waits for them, and re-layouts, local(): outbox = jnp.zeros((experts * capacity, model_width), jnp.bfloat16).at[ta...  20.1 us
  transfers between devices with their start and end apart: 2, of which 2 were waited for; matrix products, arithmetic and copies ran while one was open for 2% of the time, Pallas kernels for 0%

commit v1 on v0

v1 whole, which is shorter than its diff:
```python
import jax
import jax.numpy as jnp
from jax import lax
from jax.sharding import PartitionSpec as P

GROUP = ("expert", "replica")


def split_three(wide):
    high = wide.astype(jnp.bfloat16)
    rest = wide - high.astype(jnp.float32)
    middle = rest.astype(jnp.bfloat16)
    low = (rest - middle.astype(jnp.float32)).astype(jnp.bfloat16)
    return jnp.concatenate([high, middle, low], axis=1)


def one_chunk(tokens, expert_ids, router_weight, gate_mat, up_mat, down_mat, cotangent):
    experts = router_weight.shape[1]
    me = lax.axis_index(GROUP)
    all_tokens = lax.all_gather(tokens, GROUP, axis=0, tiled=True)
    all_ids = lax.all_gather(expert_ids, GROUP, axis=0, tiled=True)
    all_cot = lax.all_gather(cotangent, GROUP, axis=0, tiled=True)
    logits = jnp.dot(all_tokens, router_weight, preferred_element_type=jnp.float32)
    columns = jnp.arange(experts, dtype=jnp.int32)
    chosen = jnp.any(all_ids[:, :, None] == columns[None, None, :], axis=1)
    raised = jnp.where(chosen, jnp.exp(logits), 0.0)
    probs = raised / jnp.sum(raised, axis=1, keepdims=True)
    mine = jnp.sum(jnp.where(columns[None, :] == me, probs, 0.0), axis=1, keepdims=True)
    gate_act = jnp.dot(all_tokens, gate_mat, preferred_element_type=jnp.float32)
    up_act = jnp.dot(all_tokens, up_mat, preferred_element_type=jnp.float32)
    hidden = (jax.nn.silu(gate_act) * up_act).astype(jnp.bfloat16)
    out = jnp.dot(hidden, down_mat, preferred_element_type=jnp.float32).astype(jnp.bfloat16)
    out = out.astype(jnp.float32)
    dots = jnp.sum(out * all_cot.astype(jnp.float32), axis=1)
    part = jnp.where(mine > 0, mine * out, 0.0).astype(jnp.bfloat16)
    mixed = lax.psum_scatter(part, GROUP, scatter_dimension=0, tiled=True)
    slot_dots = lax.all_gather(dots, GROUP, axis=0).T
    slot_dots = jnp.where(chosen, slot_dots, 0.0)
    grad_table = probs * (slot_dots - jnp.sum(probs * slot_dots, axis=1, keepdims=True))
    pieces = lax.dot_general(
        all_tokens, split_three(grad_table), (((0,), (0,)), ((), ())), preferred_element_type=jnp.float32
    )
    grad = pieces[:, :experts] + pieces[:, experts : 2 * experts] + pieces[:, 2 * experts :]
    return mixed, grad


def local(tokens, expert_ids, router_weight, gate_weight, up_weight, down_weight, cotangent):
    rows, width = tokens.shape
    experts = router_weight.shape[1]
    chunks = max(1, experts // 16)
    mats = (gate_weight[0], up_weight[0], down_weight[0])
    if chunks == 1:
        mixed, grad = one_chunk(tokens, expert_ids, router_weight, *mats, cotangent)
    else:

        def step(total, chunk):
            mixed, grad = one_chunk(chunk[0], chunk[1], router_weight, *mats, chunk[2])
            return total + grad, mixed

        cut = lambda full: full.reshape(chunks, rows // chunks, full.shape[1])
        grad, mixed = lax.scan(
            step,
            jnp.zeros((width, experts), jnp.float32),
            (cut(tokens), cut(expert_ids), cut(cotangent)),
        )
        mixed = mixed.reshape(rows, width)
    other = lax.ppermute(grad, "dp", [(0, 1), (1, 0)])
    first = lax.axis_index("dp") == 0
    router_grad = jnp.where(first, grad, other) + jnp.where(first, other, grad)
    return (mixed, router_grad)


def solution(mesh):
    in_specs = (
        P(("dp", "expert", "replica"), None),
        P(("dp", "expert", "replica"), None),
        P(),
        P(("expert", "replica"), None, None),
        P(("expert", "replica"), None, None),
        P(("expert", "replica"), None, None),
        P(("dp", "expert", "replica"), None),
    )
    out_specs = (P(("dp", "expert", "replica"), None), P())
    return jax.shard_map(local, mesh=mesh, in_specs=in_specs, out_specs=out_specs, check_vma=False)
```

time: 857 us -> 829 us (0.967)
  waiting for transfers between devices: 412 us -> 657 us
  blocking collectives: 279 us -> 63 us
  local copies, waits for them, and re-layouts: 52.5 us -> 0.08 us
  matrix products: 52.4 us -> 80.4 us
  starting transfers between devices: 18.5 us -> 0.18 us
    reduce_scatter x0 -> x1, waiting for transfers between devices: none -> 338 us  [one_chunk(): mixed = lax.psum_scatter(part, GROUP, scatter_dimension=0, tiled=True)]
    all_gather x0 -> x2, waiting for transfers between devices: none -> 316 us  [the longest x1 162 us: one_chunk(): all_tokens = lax.all_gather(tokens, GROUP, axis=0, tiled=True)]
    all_to_all x1 -> x0, blocking collectives: 279 us -> none  [local(): lax.all_to_all(outbox, ('expert', 'replica'), split_axis=0, concat_axis=0...]
    all_to_all x1 -> x0, waiting for transfers between devices: 278 us -> none  [local(): lax.all_to_all(expert_apply(lax.all_to_all(outbox, ('expert', 'replica'),...]
    psum x1 -> x0, waiting for transfers between devices: 133 us -> none  [local(): router_grad = lax.psum(local_grad, ('dp', 'expert', 'replica'))]
    all_gather x0 -> x2, blocking collectives: none -> 63 us  [the longest x1 32.2 us: one_chunk(): slot_dots = lax.all_gather(dots, GROUP, axis=0).T]
    gather x2 -> x0, local copies, waits for them, and re-layouts: 29.2 us -> none  [the longest x1 21.4 us: local(): slot_rows = returned[target].reshape(tok_rows, top_count, model_width)]
    dot_general x8 -> x5, matrix products: 52.4 us -> 80.4 us  [the longest x1 22.3 us: one_chunk(): jnp.dot(hidden, down_mat, preferred_element_type=jnp.float32)]
  transfers between devices with their start and end apart: 2 -> 4, of which waited for: 2 -> 4; matrix products, arithmetic and copies ran while one was open for 2% -> 6% of each run, Pallas kernels for 0% -> 0%
where the time goes in v1:
time: 829 us; the launch traced here: 826 us
  waiting for transfers between devices  657 us (79%)
  matrix products  80.4 us (10%)
  blocking collectives  63 us (8%)
  between operations  13.8 us (2%)
  other arithmetic  11.4 us (1%)
    reduce_scatter x1, waiting for transfers between devices, one_chunk(): mixed = lax.psum_scatter(part, GROUP, scatter_dimension=0, tiled=True)  338 us
    all_gather x1, waiting for transfers between devices, one_chunk(): all_tokens = lax.all_gather(tokens, GROUP, axis=0, tiled=True)  162 us
    all_gather x1, waiting for transfers between devices, one_chunk(): all_cot = lax.all_gather(cotangent, GROUP, axis=0, tiled=True)  154 us
    all_gather x1, blocking collectives, one_chunk(): slot_dots = lax.all_gather(dots, GROUP, axis=0).T  32.2 us
    all_gather x1, blocking collectives, one_chunk(): all_ids = lax.all_gather(expert_ids, GROUP, axis=0, tiled=True)  30.8 us
    dot_general x1, matrix products, one_chunk(): jnp.dot(hidden, down_mat, preferred_element_type=jnp.float32)  22.3 us
    dot_general x1, matrix products, one_chunk(): gate_act = jnp.dot(all_tokens, gate_mat, preferred_element_type=jnp.float32)  19.7 us
    dot_general x1, matrix products, one_chunk(): up_act = jnp.dot(all_tokens, up_mat, preferred_element_type=jnp.float32)  19.3 us
  transfers between devices with their start and end apart: 4, of which 4 were waited for; matrix products, arithmetic and copies ran while one was open for 6% of the time, Pallas kernels for 0%

profile of v1, /device:TPU:12, one launch (start us, length us, event | category | flops | bytes accessed | tf_op | source)
XLA Modules:
  0.0 826.2 jit_solution(10628745990066714074)
XLA Ops:
  7.2 0.0 copy-start
  7.2 0.0 all-gather.4.cloned.1.call-start
  7.2 0.7 all-gather.4.cloned.1.call-update
  7.9 0.0 all-gather.6.cloned.1.call-start
  8.0 0.7 all-gather.6.cloned.1.call-update
  8.7 0.0 reduce-scatter.2.cloned.1.call-start
  8.7 30.8 %all_gather.15 = s32[2048,8]{0,1:T(8,128)S(1)} all-gather(s32[128,8]{0,1:T(8,128)} %param.8), channel_id=1, replica_groups=mesh['dp'=2,'expert'=8,'replica'=2] {'expert','replica'}, dimensions={0}, use_global_device_ids=true | all-gather | bytes 69632 | tf_op jit(solution)/shard_map/all_gather | solution.py:21
  39.5 0.1 fusion.11
  39.6 162.4 %all-gather.4.cloned.1.call-done = bf16[2048,4096]{1,0:T(8,128)(2,1)} async-done(((bf16[128,4096]{1,0:T(8,128)(2,1)}), bf16[2048,4096]{1,0:T(8,128)(2,1)}) %all-gather.4.cloned.1.call-update) | async-done | bytes 16777232 | tf_op jit(solution)/shard_map/all_gather | solution.py:20
  202.1 19.7 %fusion.6 = f32[2048,768]{1,0:T(8,128)} fusion(bf16[2048,4096]{1,0:T(8,128)(2,1)} %all-gather.4.cloned.1.call-done, bf16[1,4096,768]{2,1,0:T(8,128)(2,1)} %param.10), kind=kOutput, calls=%fused_computation.9 | convolution fusion | flops 12884901888 | bytes 29360128 | tf_op jit(solution)/shard_map/dot_general | solution.py:29
  221.7 19.3 %multiply_convert_fusion = bf16[2048,768]{1,0:T(8,128)(2,1)} fusion(f32[2048,768]{1,0:T(8,128)} %fusion.6, bf16[2048,4096]{1,0:T(8,128)(2,1)S(1)} %copy-done.1, bf16[1,4096,768]{2,1,0:T(8,128)(2,1)} %param.11), kind=kOutput, calls=%fused_computation.11 | convolution fusion | flops 12894339072 | bytes 32505856 | tf_op jit(solution)/shard_map/dot_general | solution.py:30
  241.0 153.7 %all-gather.6.cloned.1.call-done = bf16[2048,4096]{1,0:T(8,128)(2,1)} async-done(((bf16[128,4096]{1,0:T(8,128)(2,1)}), bf16[2048,4096]{1,0:T(8,128)(2,1)}) %all-gather.6.cloned.1.call-update) | async-done | bytes 16777232 | tf_op jit(solution)/shard_map/all_gather | solution.py:22
  394.6 22.3 %fusion.2 = (f32[2048]{0:T(1024)S(1)}, bf16[2048,4096]{1,0:T(8,128)(2,1)}) fusion(bf16[2048,4096]{1,0:T(8,128)(2,1)} %all-gather.6.cloned.1.call-done, bf16[2048,768]{1,0:T(8,128)(2,1)} %multiply_convert_fusion, bf16[1,768,4096]{2,1,0:T(8,128)(2,1)} %param.12), kind=kOutput, calls=%fused_computation.4 | convolution fusion | flops 12926842880 | bytes 42999808 | tf_op jit(solution)/shard_map/dot_general | solution.py:32
  417.0 32.2 %all-gather = f32[32768]{0:T(1024)S(1)} all-gather(f32[2048]{0:T(1024)S(1)} %get-tuple-element.8), channel_id=2, replica_groups=mesh['dp'=2,'expert'=8,'replica'=2] {'expert','replica'}, dimensions={0}, use_global_device_ids=true | all-gather | bytes 139264 | tf_op jit(solution)/shard_map/all_gather | solution.py:37
  449.2 10.4 %fusion.20 = (f32[2048]{0:T(1024)S(1)}, f32[2048,16]{0,1:T(8,128)S(1)}) fusion(pred[2048,16]{0,1:T(8,128)(4,1)S(1)} %fusion.11, bf16[2048,4096]{1,0:T(8,128)(2,1)} %all-gather.4.cloned.1.call-done, bf16[4096,16]{0,1:T(8,128)(2,1)S(1)} %copy-done), kind=kOutput, calls=%fused_computation.37 | convolution fusion | flops 268498944 | bytes 17080320 | tf_op jit(solution)/shard_map/dot_general | solution.py:23
  459.6 0.1 multiply_reduce_fusion
  459.7 0.0 copy-done.2
  459.8 10.3 %fusion.1 = bf16[2048,4096]{1,0:T(8,128)(2,1)} fusion(bf16[2048,4096]{1,0:T(8,128)(2,1)S(1)} %copy-done.2, f32[2048]{0:T(1024)S(1)} %get-tuple-element.3, pred[2048]{0:T(1024)(128)(4,1)S(1)} %broadcast_compare_fusion), kind=kLoop, calls=%fused_computation.3 | loop fusion | flops 33554432 | bytes 33564672 | tf_op jit(solution)/shard_map/convert_element_type | solution.py:35
  470.1 0.0 reduce-scatter.2.cloned.1.call-update
  470.2 8.8 %convolution_bitcast_fusion = f32[4096,48]{0,1:T(8,128)S(1)} fusion(bf16[2048,4096]{1,0:T(8,128)(2,1)} %all-gather.4.cloned.1.call-done, bf16[2048,16]{0,1:T(8,128)(2,1)S(1)} %get-tuple-element.7, bf16[2048,16]{0,1:T(8,128)(2,1)S(1)} %get-tuple-element.6, bf16[2048,16]{0,1:T(8,128)(2,1)S(1)} %get-tuple-element.4), kind=kOutput, calls=%fused_computation.12 | convolution fusion | flops 805896192 | bytes 17760256 | tf_op jit(solution)/shard_map/dot_general | solution.py:40
  479.0 0.1 collective-permute-start
  479.1 1.5 collective-permute-done
  480.6 0.8 select_add_fusion
  481.4 338.3 %reduce-scatter.2.cloned.1.call-done = bf16[128,4096]{1,0:T(8,128)(2,1)} async-done(((bf16[2048,4096]{1,0:T(8,128)(2,1)}), bf16[128,4096]{1,0:T(8,128)(2,1)}) %reduce-scatter.2.cloned.1.call-update) | async-done | bytes 1048592 | tf_op jit(solution)/shard_map/reduce_scatter | solution.py:36
  (10 shorter events, 0.1 us)
Async XLA Ops:
  7.2 442.0 %copy-start = (bf16[4096,16]{0,1:T(8,128)(2,1)S(1)}, bf16[4096,16]{0,1:T(8,128)(2,1)}, u32[]{:S(2)}) copy-start(bf16[4096,16]{0,1:T(8,128)(2,1)} %param.9) | copy-start | bytes 393220
  7.2 194.9 %all-gather.4.cloned.1.call-start = ((), (), s32[]{:S(2)}) async-start(), calls=%async_computation.1 | async-start | bytes 17825792 | tf_op jit(solution)/shard_map/all_gather | solution.py:20
  7.9 386.7 %all-gather.6.cloned.1.call-start = ((), (), s32[]{:S(2)}) async-start(), calls=%async_computation.3 | async-start | bytes 17825792 | tf_op jit(solution)/shard_map/all_gather | solution.py:22
  8.7 811.0 %reduce-scatter.2.cloned.1.call-start = ((), (), s32[]{:S(2)}) async-start(), calls=%async_computation.2 | async-start | bytes 17825792 | tf_op jit(solution)/shard_map/reduce_scatter | solution.py:36
  202.1 19.7 %copy-start.1 = (bf16[2048,4096]{1,0:T(8,128)(2,1)S(1)}, bf16[2048,4096]{1,0:T(8,128)(2,1)}, u32[]{:S(2)}) copy-start(bf16[2048,4096]{1,0:T(8,128)(2,1)} %all-gather.4.cloned.1.call-done) | copy-start | bytes 50331652
  449.2 10.5 %copy-start.2 = (bf16[2048,4096]{1,0:T(8,128)(2,1)S(1)}, bf16[2048,4096]{1,0:T(8,128)(2,1)}, u32[]{:S(2)}) copy-start(bf16[2048,4096]{1,0:T(8,128)(2,1)} %get-tuple-element.9) | copy-start | bytes 50331652
  479.0 1.6 collective-permute-start
Sparse Core Ops, SparseCore 0:
  10.8 191.2 all-gather.3
  204.8 189.7 all-gather.5
  470.2 349.4 reduce-scatter.1

commit v2 on v1

--- a/solution.py
+++ b/solution.py
@@ -44,9 +44,119 @@
     return mixed, grad
 
 
+def paired(tokens, expert_ids, router_weight, gate_weight, up_weight, down_weight, cotangent, layers):
+    rows, width = tokens.shape
+    experts = router_weight.shape[1]
+    units = gate_weight.shape[2]
+    place = lax.axis_index("expert")
+    layer, side = place // 2, place % 2
+    copy = lax.axis_index("replica")
+    core = lax.axis_index("dp")
+    half = units // 2
+
+    def shift(block, step):
+        pairs = [(z * 2 + x, (z + step) % layers * 2 + x) for z in range(layers) for x in range(2)]
+        return lax.ppermute(block, "expert", pairs)
+
+    def swap(block):
+        return lax.ppermute(block, "expert", [(e, e ^ 1) for e in range(2 * layers)])
+
+    def across(block, axis):
+        return lax.ppermute(block, axis, [(0, 1), (1, 0)])
+
+    def spread(block):
+        near = [block] + [shift(block, step) for step in range(1, layers)]
+        return [near, [swap(one) for one in near]]
+
+    first_half = core * half
+    sent = (
+        lax.dynamic_slice(gate_weight[0], (0, first_half), (width, half)),
+        lax.dynamic_slice(up_weight[0], (0, first_half), (width, half)),
+        lax.dynamic_slice(down_weight[0], (first_half, 0), (half, width)),
+    )
+    fetched = [across(part, "replica") for part in sent]
+    second = [
+        jnp.concatenate([part, across(part, "dp")], axis=axis) for part, axis in zip(fetched, (1, 1, 0))
+    ]
+    mats = [(gate_weight[0], up_weight[0], down_weight[0]), tuple(second)]
+
+    logits = jnp.dot(tokens, router_weight, preferred_element_type=jnp.float32)
+    columns = jnp.arange(experts, dtype=jnp.int32)
+    chosen = jnp.any(expert_ids[:, :, None] == columns[None, None, :], axis=1)
+    raised = jnp.where(chosen, jnp.exp(logits), 0.0)
+    own_probs = raised / jnp.sum(raised, axis=1, keepdims=True)
+
+    token_blocks = spread(tokens)
+    prob_blocks = spread(own_probs)
+    cotangent, _ = lax.optimization_barrier((cotangent, token_blocks[0][layers - 1]))
+    cot_blocks = spread(cotangent)
+    token_sides = [jnp.concatenate(blocks, axis=0) for blocks in token_blocks]
+    prob_sides = [jnp.concatenate(blocks, axis=0) for blocks in prob_blocks]
+    cot_sides = [jnp.concatenate(blocks, axis=0) for blocks in cot_blocks]
+
+    def expert_on(which, x):
+        gate_mat, up_mat, down_mat = mats[which]
+        gate_act = jnp.dot(token_sides[x], gate_mat, preferred_element_type=jnp.float32)
+        up_act = jnp.dot(token_sides[x], up_mat, preferred_element_type=jnp.float32)
+        hidden = (jax.nn.silu(gate_act) * up_act).astype(jnp.bfloat16)
+        out = jnp.dot(hidden, down_mat, preferred_element_type=jnp.float32).astype(jnp.bfloat16)
+        out = out.astype(jnp.float32)
+        name = place * 2 + (copy if which == 0 else 1 - copy)
+        mine = jnp.sum(jnp.where(columns[None, :] == name, prob_sides[x], 0.0), axis=1, keepdims=True)
+        return mine * out, jnp.sum(out * cot_sides[x].astype(jnp.float32), axis=1)
+
+    own = [expert_on(0, x) for x in range(2)]
+    other = [None, None]
+    other[1] = expert_on(1, 1)
+    far = (own[1][0] + other[1][0]).astype(jnp.bfloat16).reshape(layers, rows, width)
+    arrived = [swap(far[step]) for step in range(layers)]
+    other[0] = expert_on(1, 0)
+    near = (own[0][0] + other[0][0]).reshape(layers, rows, width)
+    sums = [near[step] + arrived[step].astype(jnp.float32) for step in range(layers)]
+    mixed = sums[0]
+    for step in range(1, layers):
+        mixed = mixed + shift(sums[step].astype(jnp.bfloat16), -step).astype(jnp.float32)
+    mixed = mixed.astype(jnp.bfloat16)
+
+    dots = jnp.stack(
+        [jnp.stack([own[x][1] for x in range(2)]), jnp.stack([other[x][1] for x in range(2)])]
+    ).reshape(2, 2, layers, rows)
+    dot_blocks = spread(dots.reshape(4 * layers, rows))
+    table = jnp.zeros((2 * layers * rows, experts), jnp.float32)
+    for x in range(2):
+        for step in range(layers):
+            block = dot_blocks[x][step].reshape(2, 2, layers, rows)
+            block = jnp.roll(jnp.flip(block, 1) if x else block, step, axis=2).reshape(2, -1)
+            there = ((layer - step) % layers * 2 + (side ^ x)) * 2
+            for which in range(2):
+                name = there + (copy if which == 0 else 1 - copy)
+                table = jnp.where(columns[None, :] == name, block[which][:, None], table)
+    probs = jnp.concatenate(prob_sides, axis=0)
+    grad_table = probs * (table - jnp.sum(probs * table, axis=1, keepdims=True))
+    part = width // (2 * layers)
+    strip = jnp.concatenate(
+        [lax.dynamic_slice(side_rows, (0, place * part), (layers * rows, part)) for side_rows in token_sides]
+    )
+    pieces = lax.dot_general(
+        strip, split_three(grad_table), (((0,), (0,)), ((), ())), preferred_element_type=jnp.float32
+    )
+    grad = pieces[:, :experts] + pieces[:, experts : 2 * experts] + pieces[:, 2 * experts :]
+    grad = grad + across(grad, "replica")
+    grad = grad + across(grad, "dp")
+    strips = jnp.stack([jnp.stack(blocks) for blocks in spread(grad.reshape(part * experts // 128, 128))])
+    whose = jnp.arange(2 * layers, dtype=jnp.int32)
+    from_side, from_layer = (whose % 2) ^ side, (layer - whose // 2) % layers
+    router_grad = strips.reshape(2 * layers, -1)[from_side * layers + from_layer].reshape(width, experts)
+    return mixed, router_grad
+
+
 def local(tokens, expert_ids, router_weight, gate_weight, up_weight, down_weight, cotangent):
     rows, width = tokens.shape
     experts = router_weight.shape[1]
+    if lax.axis_size("expert") == 8 and lax.axis_size("replica") == 2:
+        return paired(
+            tokens, expert_ids, router_weight, gate_weight, up_weight, down_weight, cotangent, 4
+        )
     chunks = max(1, experts // 16)
     mats = (gate_weight[0], up_weight[0], down_weight[0])
     if chunks == 1:

time: 829 us -> 597 us (0.72)
  waiting for transfers between devices: 657 us -> 379 us
  blocking collectives: 63 us -> 0 us
  starting transfers between devices: 0.18 us -> 48.1 us
  local copies, waits for them, and re-layouts: 0.08 us -> 43.4 us
  matrix products: 80.4 us -> 105 us
  between operations: 13.8 us -> 1.62 us
    ppermute x1 -> x50, waiting for transfers between devices: 1.52 us -> 379 us  [the longest x24 177 us: swap(): lax.ppermute(block, 'expert', [(e, e ^ 1) for e in range(2 * layers)])]
    reduce_scatter x1 -> x0, waiting for transfers between devices: 338 us -> none  [one_chunk(): mixed = lax.psum_scatter(part, GROUP, scatter_dimension=0, tiled=True)]
    all_gather x2 -> x0, waiting for transfers between devices: 316 us -> none  [the longest x1 162 us: one_chunk(): all_tokens = lax.all_gather(tokens, GROUP, axis=0, tiled=True)]
    all_gather x2 -> x0, blocking collectives: 63 us -> none  [the longest x1 32.2 us: one_chunk(): slot_dots = lax.all_gather(dots, GROUP, axis=0).T]
    ppermute x1 -> x50, starting transfers between devices: 0.07 us -> 48.1 us  [the longest x24 25.6 us: swap(): lax.ppermute(block, 'expert', [(e, e ^ 1) for e in range(2 * layers)])]
    dot_general x5 -> x10, matrix products: 80.4 us -> 105 us  [the longest x4 73.6 us: expert_on(): jnp.dot(hidden, down_mat, preferred_element_type=jnp.float32)]
    unnamed x6 -> x77, local copies, waits for them, and re-layouts: 0.06 us -> 18.7 us
    dynamic_slice x0 -> x5, local copies, waits for them, and re-layouts: none -> 10.8 us  [the longest x1 4.07 us: paired(): lax.dynamic_slice(gate_weight[0], (0, first_half), (width, half))]
  transfers between devices with their start and end apart: 4 -> 50, of which waited for: 4 -> 25; matrix products, arithmetic and copies ran while one was open for 6% -> 22% of each run, Pallas kernels for 0% -> 0%
where the time goes in v2:
time: 597 us; the launch traced here: 592 us
  waiting for transfers between devices  379 us (63%)
  matrix products  105 us (18%)
  starting transfers between devices  48.1 us (8%)
  local copies, waits for them, and re-layouts  43.4 us (7%)
  other arithmetic  15.3 us (3%)
    ppermute x24, waiting for transfers between devices, swap(): lax.ppermute(block, 'expert', [(e, e ^ 1) for e in range(2 * layers)])  177 us
    ppermute x18, waiting for transfers between devices, shift(): return lax.ppermute(block, 'expert', pairs)  147 us
    dot_general x4, matrix products, expert_on(): jnp.dot(hidden, down_mat, preferred_element_type=jnp.float32)  73.6 us
    ppermute x8, waiting for transfers between devices, across(): return lax.ppermute(block, axis, [(0, 1), (1, 0)])  54.2 us
    ppermute x24, starting transfers between devices, swap(): lax.ppermute(block, 'expert', [(e, e ^ 1) for e in range(2 * layers)])  25.6 us
    ppermute x18, starting transfers between devices, shift(): return lax.ppermute(block, 'expert', pairs)  20.3 us
    unnamed x77, local copies, waits for them, and re-layouts  18.7 us
    dot_general x2, matrix products, expert_on(): up_act = jnp.dot(token_sides[x], up_mat, preferred_element_type=jnp.float32)  16.8 us
  transfers between devices with their start and end apart: 50, of which 25 were waited for; matrix products, arithmetic and copies ran while one was open for 22% of the time, Pallas kernels for 0%

profile of v2, /device:TPU:12, one launch (start us, length us, event | category | flops | bytes accessed | tf_op | source)
XLA Modules:
  0.0 592.3 jit_solution(2498507991957035704)
XLA Ops:
  33.0 18.0 %collective-permute-done.13 = f32[128,16]{0,1:T(8,128)S(1)} collective-permute-done((f32[128,16]{0,1:T(8,128)S(1)}, f32[128,16]{0,1:T(8,128)S(1)}, u32[]{:S(2)}, u32[]{:S(2)}) %collective-permute-start.13) | collective-permute-done | bytes 8224 | tf_op jit(solution)/shard_map/ppermute | solution.py:62
  58.9 19.1 %collective-permute-done.3 = bf16[128,4096]{1,0:T(8,128)(2,1)S(1)} collective-permute-done((bf16[128,4096]{1,0:T(8,128)(2,1)}, bf16[128,4096]{1,0:T(8,128)(2,1)S(1)}, u32[]{:S(2)}, u32[]{:S(2)}) %collective-permute-start.3) | collective-permute-done | bytes 1048608 | tf_op jit(solution)/shard_map/ppermute | solution.py:59
  79.6 19.2 %collective-permute-done.4 = bf16[128,4096]{1,0:T(8,128)(2,1)} collective-permute-done((bf16[128,4096]{1,0:T(8,128)(2,1)S(1)}, bf16[128,4096]{1,0:T(8,128)(2,1)}, u32[]{:S(2)}, u32[]{:S(2)}) %collective-permute-start.4) | collective-permute-done | bytes 1048608 | tf_op jit(solution)/shard_map/ppermute | solution.py:59
  104.9 8.7 %fusion.13 = f32[512,768]{1,0:T(8,128)} fusion(bf16[512,4096]{1,0:T(8,128)(2,1)} %constant_dynamic-update-slice_fusion, bf16[1,4096,768]{2,1,0:T(8,128)(2,1)} %param.11), kind=kOutput, calls=%fused_computation.22 | convolution fusion | flops 3221225472 | bytes 12058624 | tf_op jit(solution)/shard_map/dot_general | solution.py:100
  114.0 17.1 %fusion.19 = bf16[512,4096]{1,0:T(8,128)(2,1)} fusion(bf16[1,768,4096]{2,1,0:T(8,128)(2,1)} %param.12, f32[512,768]{1,0:T(8,128)} %fusion.13, bf16[512,4096]{1,0:T(8,128)(2,1)} %constant_dynamic-update-slice_fusion, bf16[1,4096,768]{2,1,0:T(8,128)(2,1)} %param.10), kind=kOutput, calls=%fused_computation.28 | convolution fusion | flops 6446907392 | bytes 22544384 | tf_op jit(solution)/shard_map/dot_general | solution.py:102
  135.2 4.5 collective-permute-done.17
  141.5 20.6 %collective-permute-done.18 = bf16[128,4096]{1,0:T(8,128)(2,1)S(1)} collective-permute-done((bf16[128,4096]{1,0:T(8,128)(2,1)}, bf16[128,4096]{1,0:T(8,128)(2,1)S(1)}, u32[]{:S(2)}, u32[]{:S(2)}) %collective-permute-start.18) | collective-permute-done | bytes 1048608 | tf_op jit(solution)/shard_map/ppermute | solution.py:62
  162.3 21.2 %collective-permute-done.19 = bf16[128,4096]{1,0:T(8,128)(2,1)S(1)} collective-permute-done((bf16[128,4096]{1,0:T(8,128)(2,1)}, bf16[128,4096]{1,0:T(8,128)(2,1)S(1)}, u32[]{:S(2)}, u32[]{:S(2)}) %collective-permute-start.19) | collective-permute-done | bytes 1048608 | tf_op jit(solution)/shard_map/ppermute | solution.py:62
  183.9 8.1 %fusion.11 = f32[512,768]{1,0:T(8,128)} fusion(bf16[512,4096]{1,0:T(8,128)(2,1)S(1)} %constant_dynamic-update-slice_fusion.14, bf16[1,4096,768]{2,1,0:T(8,128)(2,1)} %param.11), kind=kOutput, calls=%fused_computation.20 | convolution fusion | flops 3221225472 | bytes 12058624 | tf_op jit(solution)/shard_map/dot_general | solution.py:100
  197.1 17.1 %fusion.22 = bf16[512,4096]{1,0:T(8,128)(2,1)} fusion(bf16[1,768,4096]{2,1,0:T(8,128)(2,1)} %param.12, f32[512,768]{1,0:T(8,128)} %fusion.11, bf16[512,4096]{1,0:T(8,128)(2,1)} %copy-done.9, bf16[1,4096,768]{2,1,0:T(8,128)(2,1)} %param.10), kind=kOutput, calls=%fused_computation.29 | convolution fusion | flops 6446907392 | bytes 22544384 | tf_op jit(solution)/shard_map/dot_general | solution.py:102
  214.1 45.5 %collective-permute-done.10 = bf16[384,4096]{1,0:T(8,128)(2,1)S(1)} collective-permute-done((bf16[384,4096]{1,0:T(8,128)(2,1)}, bf16[384,4096]{1,0:T(8,128)(2,1)S(1)}, u32[]{:S(2)}, u32[]{:S(2)}) %collective-permute-start.10) | collective-permute-done | bytes 3145760 | tf_op jit(solution)/shard_map/ppermute | solution.py:65
  270.4 19.5 %collective-permute-done.29 = bf16[128,4096]{1,0:T(8,128)(2,1)} collective-permute-done((bf16[128,4096]{1,0:T(8,128)(2,1)}, bf16[128,4096]{1,0:T(8,128)(2,1)}, u32[]{:S(2)}, u32[]{:S(2)}) %collective-permute-start.29) | collective-permute-done | bytes 1048608 | tf_op jit(solution)/shard_map/ppermute | solution.py:59
  294.5 4.6 fusion.87
  302.1 20.3 %fusion.4 = (f32[512]{0:T(512)S(1)}, f32[512]{0:T(512)S(1)}, f32[512,4096]{1,0:T(8,128)}) fusion(bf16[128,4096]{1,0:T(8,128)(2,1)} %collective-permute-done.29, bf16[128,4096]{1,0:T(8,128)(2,1)} %collective-permute-done.28, bf16[128,4096]{1,0:T(8,128)(2,1)} %collective-permute-done.27, bf16[128,4096]{1,0:T(8,128)(2,1)} %param.13, ...), kind=kOutput, calls=%fused_computation.13 | convolution fusion | flops 6482557952 | bytes 35135488 | tf_op jit(solution)/shard_map/dot_general | solution.py:102
  322.3 7.0 %fusion.88 = f32[512,768]{1,0:T(8,128)S(1)} fusion(bf16[512,4096]{1,0:T(8,128)(2,1)} %copy-done.9, bf16[4096,768]{1,0:T(8,128)(2,1)} %copy-done.7), kind=kOutput, calls=%fused_computation.193 | convolution fusion | flops 3221225472 | bytes 12058624 | tf_op jit(solution)/shard_map/dot_general | solution.py:99
  329.4 10.3 %collective-permute-done.32 = bf16[128,4096]{1,0:T(8,128)(2,1)} collective-permute-done((bf16[128,4096]{1,0:T(8,128)(2,1)}, bf16[128,4096]{1,0:T(8,128)(2,1)}, u32[]{:S(2)}, u32[]{:S(2)}) %collective-permute-start.32) | collective-permute-done | bytes 1048608 | tf_op jit(solution)/shard_map/ppermute | solution.py:62
  339.7 21.8 %collective-permute-done.33 = bf16[128,4096]{1,0:T(8,128)(2,1)} collective-permute-done((bf16[128,4096]{1,0:T(8,128)(2,1)}, bf16[128,4096]{1,0:T(8,128)(2,1)}, u32[]{:S(2)}, u32[]{:S(2)}) %collective-permute-start.33) | collective-permute-done | bytes 1048608 | tf_op jit(solution)/shard_map/ppermute | solution.py:62
  361.4 19.2 %fusion.6 = (f32[512]{0:T(512)S(1)}, f32[512]{0:T(512)S(1)}, bf16[512,4096]{1,0:T(8,128)(2,1)}) fusion(bf16[128,4096]{1,0:T(8,128)(2,1)} %collective-permute-done.33, bf16[128,4096]{1,0:T(8,128)(2,1)} %collective-permute-done.32, bf16[128,4096]{1,0:T(8,128)(2,1)} %collective-permute-done.31, bf16[128,4096]{1,0:T(8,128)(2,1)} %collective-permute-done.30, ...), kind=kOutput, calls=%fused_computation.15 | convolution fusion | flops 6484655104 | bytes 30941184 | tf_op jit(solution)/shard_map/dot_general | solution.py:102
  385.7 4.4 fusion.78
  396.0 63.3 %collective-permute-done.37 = f32[16,128]{1,0:T(8,128)S(1)} collective-permute-done((f32[16,128]{1,0:T(8,128)S(1)}, f32[16,128]{1,0:T(8,128)S(1)}, u32[]{:S(2)}, u32[]{:S(2)}) %collective-permute-start.37) | collective-permute-done | bytes 8224 | tf_op jit(solution)/shard_map/ppermute | solution.py:62
  465.1 5.2 fusion.27
  480.2 79.8 %collective-permute-done.43 = f32[64,128]{1,0:T(8,128)S(1)} collective-permute-done((f32[64,128]{1,0:T(8,128)S(1)}, f32[64,128]{1,0:T(8,128)S(1)}, u32[]{:S(2)}, u32[]{:S(2)}) %collective-permute-start.43) | collective-permute-done | bytes 32800 | tf_op jit(solution)/shard_map/ppermute | solution.py:59
  560.0 4.8 collective-permute-done.44
  587.9 4.2 fusion.31
  (232 shorter events, 127.4 us)
Async XLA Ops:
  9.4 68.6 %collective-permute-start.3 = (bf16[128,4096]{1,0:T(8,128)(2,1)}, bf16[128,4096]{1,0:T(8,128)(2,1)S(1)}, u32[]{:S(2)}, u32[]{:S(2)}) collective-permute-start(bf16[128,4096]{1,0:T(8,128)(2,1)} %param.7), channel_id=1, source_target_pairs={{0,4},{2,6},{4,8},{6,10},{8,12},{10,14},{12,0},{14,2},{1,5},{3,7},... | collective-permute-start | bytes 3145736 | tf_op jit(solution)/shard_map/ppermute | solution.py:59
  27.2 105.5 %collective-permute-start.16 = (bf16[128,4096]{1,0:T(8,128)(2,1)S(1)}, bf16[128,4096]{1,0:T(8,128)(2,1)S(1)}, u32[]{:S(2)}, u32[]{:S(2)}) collective-permute-start(bf16[128,4096]{1,0:T(8,128)(2,1)S(1)} %copy-done.2), channel_id=1, source_target_pairs={{0,2},{2,0},{4,6},{6,4},{8,10},{10,8},{12,14},{14,12},{1,3},{3,1},... | collective-permute-start | bytes 3145736 | tf_op jit(solution)/shard_map/ppermute | solution.py:62
  27.7 71.0 %collective-permute-start.4 = (bf16[128,4096]{1,0:T(8,128)(2,1)S(1)}, bf16[128,4096]{1,0:T(8,128)(2,1)}, u32[]{:S(2)}, u32[]{:S(2)}) collective-permute-start(bf16[128,4096]{1,0:T(8,128)(2,1)S(1)} %copy-done.2), channel_id=1, source_target_pairs={{0,8},{2,10},{4,12},{6,14},{8,0},{10,2},{12,4},{14,6},{1,9},{3,11}... | collective-permute-start | bytes 3145736 | tf_op jit(solution)/shard_map/ppermute | solution.py:59
  31.2 71.4 %collective-permute-start.5 = (bf16[128,4096]{1,0:T(8,128)(2,1)S(1)}, bf16[128,4096]{1,0:T(8,128)(2,1)}, u32[]{:S(2)}, u32[]{:S(2)}) collective-permute-start(bf16[128,4096]{1,0:T(8,128)(2,1)S(1)} %copy-done.2), channel_id=1, source_target_pairs={{0,12},{2,14},{4,0},{6,2},{8,4},{10,6},{12,8},{14,10},{1,13},{3,15... | collective-permute-start | bytes 3145736 | tf_op jit(solution)/shard_map/ppermute | solution.py:59
  58.3 125.6 %collective-permute-start.6 = (bf16[4096,384]{1,0:T(8,128)(2,1)}, bf16[4096,384]{1,0:T(8,128)(2,1)}, u32[]{:S(2)}, u32[]{:S(2)}) collective-permute-start(bf16[4096,384]{1,0:T(8,128)(2,1)} %dynamic-slice_bitcast_fusion.2), channel_id=1, source_target_pairs={{0,1},{1,0},{2,3},{3,2},{4,5},{5,4},{6,7},{7,6},{8,9},{9,8},{10,11... | collective-permute-start | bytes 9437192 | tf_op jit(solution)/shard_map/ppermute | solution.py:65
  78.0 119.1 %collective-permute-start.8 = (bf16[4096,384]{1,0:T(8,128)(2,1)}, bf16[4096,384]{1,0:T(8,128)(2,1)}, u32[]{:S(2)}, u32[]{:S(2)}) collective-permute-start(bf16[4096,384]{1,0:T(8,128)(2,1)} %dynamic-slice_bitcast_fusion.1), channel_id=1, source_target_pairs={{0,1},{1,0},{2,3},{3,2},{4,5},{5,4},{6,7},{7,6},{8,9},{9,8},{10,11... | collective-permute-start | bytes 9437192 | tf_op jit(solution)/shard_map/ppermute | solution.py:65
  139.7 119.9 %collective-permute-start.10 = (bf16[384,4096]{1,0:T(8,128)(2,1)}, bf16[384,4096]{1,0:T(8,128)(2,1)S(1)}, u32[]{:S(2)}, u32[]{:S(2)}) collective-permute-start(bf16[384,4096]{1,0:T(8,128)(2,1)} %dynamic-slice_bitcast_fusion), channel_id=1, source_target_pairs={{0,1},{1,0},{2,3},{3,2},{4,5},{5,4},{6,7},{7,6},{8,9},{9,8},{10,11... | collective-permute-start | bytes 9437192 | tf_op jit(solution)/shard_map/ppermute | solution.py:65
  162.1 106.3 %collective-permute-start.27 = (bf16[128,4096]{1,0:T(8,128)(2,1)}, bf16[128,4096]{1,0:T(8,128)(2,1)}, u32[]{:S(2)}, u32[]{:S(2)}) collective-permute-start(bf16[128,4096]{1,0:T(8,128)(2,1)} %param.13), channel_id=1, source_target_pairs={{0,4},{2,6},{4,8},{6,10},{8,12},{10,14},{12,0},{14,2},{1,5},{3,7},... | collective-permute-start | bytes 3145736 | tf_op jit(solution)/shard_map/ppermute | solution.py:59
  183.6 85.4 %collective-permute-start.28 = (bf16[128,4096]{1,0:T(8,128)(2,1)}, bf16[128,4096]{1,0:T(8,128)(2,1)}, u32[]{:S(2)}, u32[]{:S(2)}) collective-permute-start(bf16[128,4096]{1,0:T(8,128)(2,1)} %param.13), channel_id=1, source_target_pairs={{0,8},{2,10},{4,12},{6,14},{8,0},{10,2},{12,4},{14,6},{1,9},{3,11}... | collective-permute-start | bytes 3145736 | tf_op jit(solution)/shard_map/ppermute | solution.py:59
  183.9 80.1 %collective-permute-start.7 = (bf16[4096,384]{1,0:T(8,128)(2,1)}, bf16[4096,384]{1,0:T(8,128)(2,1)}, u32[]{:S(2)}, u32[]{:S(2)}) collective-permute-start(bf16[4096,384]{1,0:T(8,128)(2,1)} %collective-permute-done.6), channel_id=1, source_target_pairs={{0,16},{16,0},{1,17},{17,1},{2,18},{18,2},{3,19},{19,3},{4,20},{20... | collective-permute-start | bytes 9437192 | tf_op jit(solution)/shard_map/ppermute | solution.py:65
  197.0 93.4 %collective-permute-start.9 = (bf16[4096,384]{1,0:T(8,128)(2,1)}, bf16[4096,384]{1,0:T(8,128)(2,1)}, u32[]{:S(2)}, u32[]{:S(2)}) collective-permute-start(bf16[4096,384]{1,0:T(8,128)(2,1)} %collective-permute-done.8), channel_id=1, source_target_pairs={{0,16},{16,0},{1,17},{17,1},{2,18},{18,2},{3,19},{19,3},{4,20},{20... | collective-permute-start | bytes 9437192 | tf_op jit(solution)/shard_map/ppermute | solution.py:65
  268.4 61.0 %collective-permute-start.30 = (bf16[128,4096]{1,0:T(8,128)(2,1)}, bf16[128,4096]{1,0:T(8,128)(2,1)}, u32[]{:S(2)}, u32[]{:S(2)}) collective-permute-start(bf16[128,4096]{1,0:T(8,128)(2,1)} %param.13), channel_id=1, source_target_pairs={{0,2},{2,0},{4,6},{6,4},{8,10},{10,8},{12,14},{14,12},{1,3},{3,1},... | collective-permute-start | bytes 3145736 | tf_op jit(solution)/shard_map/ppermute | solution.py:62
  269.0 60.4 %collective-permute-start.31 = (bf16[128,4096]{1,0:T(8,128)(2,1)}, bf16[128,4096]{1,0:T(8,128)(2,1)}, u32[]{:S(2)}, u32[]{:S(2)}) collective-permute-start(bf16[128,4096]{1,0:T(8,128)(2,1)} %collective-permute-done.27), channel_id=1, source_target_pairs={{0,2},{2,0},{4,6},{6,4},{8,10},{10,8},{12,14},{14,12},{1,3},{3,1},... | collective-permute-start | bytes 3145736 | tf_op jit(solution)/shard_map/ppermute | solution.py:62
  290.5 70.9 %collective-permute-start.33 = (bf16[128,4096]{1,0:T(8,128)(2,1)}, bf16[128,4096]{1,0:T(8,128)(2,1)}, u32[]{:S(2)}, u32[]{:S(2)}) collective-permute-start(bf16[128,4096]{1,0:T(8,128)(2,1)} %collective-permute-done.29), channel_id=1, source_target_pairs={{0,2},{2,0},{4,6},{6,4},{8,10},{10,8},{12,14},{14,12},{1,3},{3,1},... | collective-permute-start | bytes 3145736 | tf_op jit(solution)/shard_map/ppermute | solution.py:62
  390.1 74.9 %collective-permute-start.21 = (bf16[128,4096]{1,0:T(8,128)(2,1)}, bf16[128,4096]{1,0:T(8,128)(2,1)S(1)}, u32[]{:S(2)}, u32[]{:S(2)}) collective-permute-start(bf16[128,4096]{1,0:T(8,128)(2,1)} %get-tuple-element.32), channel_id=1, source_target_pairs={{0,2},{2,0},{4,6},{6,4},{8,10},{10,8},{12,14},{14,12},{1,3},{3,1},... | collective-permute-start | bytes 3145736 | tf_op jit(solution)/shard_map/ppermute | solution.py:62
  391.6 73.5 %collective-permute-start.23 = (bf16[128,4096]{1,0:T(8,128)(2,1)}, bf16[128,4096]{1,0:T(8,128)(2,1)S(1)}, u32[]{:S(2)}, u32[]{:S(2)}) collective-permute-start(bf16[128,4096]{1,0:T(8,128)(2,1)} %get-tuple-element.31), channel_id=1, source_target_pairs={{0,2},{2,0},{4,6},{6,4},{8,10},{10,8},{12,14},{14,12},{1,3},{3,1},... | collective-permute-start | bytes 3145736 | tf_op jit(solution)/shard_map/ppermute | solution.py:62
  392.1 72.9 %collective-permute-start.25 = (bf16[128,4096]{1,0:T(8,128)(2,1)}, bf16[128,4096]{1,0:T(8,128)(2,1)}, u32[]{:S(2)}, u32[]{:S(2)}) collective-permute-start(bf16[128,4096]{1,0:T(8,128)(2,1)} %get-tuple-element.30), channel_id=1, source_target_pairs={{0,2},{2,0},{4,6},{6,4},{8,10},{10,8},{12,14},{14,12},{1,3},{3,1},... | collective-permute-start | bytes 3145736 | tf_op jit(solution)/shard_map/ppermute | solution.py:62
  393.8 65.4 %collective-permute-start.37 = (f32[16,128]{1,0:T(8,128)S(1)}, f32[16,128]{1,0:T(8,128)S(1)}, u32[]{:S(2)}, u32[]{:S(2)}) collective-permute-start(f32[16,128]{1,0:T(8,128)S(1)} %collective-permute-done.36), channel_id=1, source_target_pairs={{0,2},{2,0},{4,6},{6,4},{8,10},{10,8},{12,14},{14,12},{1,3},{3,1},... | collective-permute-start | bytes 24584 | tf_op jit(solution)/shard_map/ppermute | solution.py:62
  394.4 66.3 %collective-permute-start.35 = (f32[16,128]{1,0:T(8,128)S(1)}, f32[16,128]{1,0:T(8,128)S(1)}, u32[]{:S(2)}, u32[]{:S(2)}) collective-permute-start(f32[16,128]{1,0:T(8,128)S(1)} %collective-permute-done.34), channel_id=1, source_target_pairs={{0,2},{2,0},{4,6},{6,4},{8,10},{10,8},{12,14},{14,12},{1,3},{3,1},... | collective-permute-start | bytes 24584 | tf_op jit(solution)/shard_map/ppermute | solution.py:62
  460.7 127.2 %collective-permute-start.20 = (bf16[128,4096]{1,0:T(8,128)(2,1)}, bf16[128,4096]{1,0:T(8,128)(2,1)S(1)}, u32[]{:S(2)}, u32[]{:S(2)}) collective-permute-start(bf16[128,4096]{1,0:T(8,128)(2,1)} %get-tuple-element.29), channel_id=1, source_target_pairs={{0,2},{2,0},{4,6},{6,4},{8,10},{10,8},{12,14},{14,12},{1,3},{3,1},... | collective-permute-start | bytes 3145736 | tf_op jit(solution)/shard_map/ppermute | solution.py:62
  470.3 117.6 %collective-permute-start.22 = (bf16[128,4096]{1,0:T(8,128)(2,1)}, bf16[128,4096]{1,0:T(8,128)(2,1)}, u32[]{:S(2)}, u32[]{:S(2)}) collective-permute-start(bf16[128,4096]{1,0:T(8,128)(2,1)} %get-tuple-element.26), channel_id=1, source_target_pairs={{0,12},{2,14},{4,0},{6,2},{8,4},{10,6},{12,8},{14,10},{1,13},{3,15... | collective-permute-start | bytes 3145736 | tf_op jit(solution)/shard_map/ppermute | solution.py:59
  470.5 117.4 %collective-permute-start.24 = (bf16[128,4096]{1,0:T(8,128)(2,1)}, bf16[128,4096]{1,0:T(8,128)(2,1)}, u32[]{:S(2)}, u32[]{:S(2)}) collective-permute-start(bf16[128,4096]{1,0:T(8,128)(2,1)} %get-tuple-element.28), channel_id=1, source_target_pairs={{0,8},{2,10},{4,12},{6,14},{8,0},{10,2},{12,4},{14,6},{1,9},{3,11}... | collective-permute-start | bytes 3145736 | tf_op jit(solution)/shard_map/ppermute | solution.py:59
  473.2 114.7 %collective-permute-start.26 = (bf16[128,4096]{1,0:T(8,128)(2,1)}, bf16[128,4096]{1,0:T(8,128)(2,1)}, u32[]{:S(2)}, u32[]{:S(2)}) collective-permute-start(bf16[128,4096]{1,0:T(8,128)(2,1)} %get-tuple-element.27), channel_id=1, source_target_pairs={{0,4},{2,6},{4,8},{6,10},{8,12},{10,14},{12,0},{14,2},{1,5},{3,7},... | collective-permute-start | bytes 3145736 | tf_op jit(solution)/shard_map/ppermute | solution.py:59
  480.2 79.8 %collective-permute-start.43 = (f32[64,128]{1,0:T(8,128)S(1)}, f32[64,128]{1,0:T(8,128)S(1)}, u32[]{:S(2)}, u32[]{:S(2)}) collective-permute-start(f32[64,128]{1,0:T(8,128)S(1)} %reshape.320), channel_id=1, source_target_pairs={{0,4},{2,6},{4,8},{6,10},{8,12},{10,14},{12,0},{14,2},{1,5},{3,7},... | collective-permute-start | bytes 98312 | tf_op jit(solution)/shard_map/ppermute | solution.py:59
  (55 other events, 1888.7 us)

commit v3 on v1

--- a/solution.py
+++ b/solution.py
@@ -44,9 +44,147 @@
     return mixed, grad
 
 
+def paired(tokens, expert_ids, router_weight, gate_weight, up_weight, down_weight, cotangent, layers):
+    rows, width = tokens.shape
+    experts = router_weight.shape[1]
+    units = gate_weight.shape[2]
+    place = lax.axis_index("expert")
+    layer, side = place // 2, place % 2
+    copy = lax.axis_index("replica")
+    core = lax.axis_index("dp")
+    half = units // 2
+
+    def shift(block, step):
+        pairs = [(z * 2 + x, (z + step) % layers * 2 + x) for z in range(layers) for x in range(2)]
+        return lax.ppermute(block, "expert", pairs)
+
+    def swap(block):
+        return lax.ppermute(block, "expert", [(e, e ^ 1) for e in range(2 * layers)])
+
+    def across(block, axis):
+        return lax.ppermute(block, axis, [(0, 1), (1, 0)])
+
+    def follow(block, after):
+        return block if after is None else lax.optimization_barrier((block, after))[0]
+
+    def spread(block, shifts, swaps):
+        near = [block] + [shift(follow(block, shifts.get(step)), step) for step in range(1, layers)]
+        return [near, [swap(follow(one, swaps.get(step))) for step, one in enumerate(near)]]
+
+    first_half = core * half
+    sent = (
+        lax.dynamic_slice(gate_weight[0], (0, first_half), (width, half)),
+        lax.dynamic_slice(up_weight[0], (0, first_half), (width, half)),
+        lax.dynamic_slice(down_weight[0], (first_half, 0), (half, width)),
+    )
+    fetched = [across(sent[0], "replica"), None, across(sent[2], "replica")]
+    later, _ = lax.optimization_barrier((sent[1], fetched[2]))
+    fetched[1] = across(later, "replica")
+    second = [
+        jnp.concatenate([part, across(part, "dp")], axis=axis) for part, axis in zip(fetched, (1, 1, 0))
+    ]
+    mats = [(gate_weight[0], up_weight[0], down_weight[0]), tuple(second)]
+
+    columns = jnp.arange(experts, dtype=jnp.int32)
+    chosen = jnp.any(expert_ids[:, :, None] == columns[None, None, :], axis=1)
+    marks = jnp.pad(chosen.astype(jnp.bfloat16), ((0, 0), (0, -experts % 128)))
+    marked = jnp.concatenate([tokens, marks], axis=1)
+    marked, _ = lax.optimization_barrier((marked, sent[2]))
+    token_blocks = spread(marked, {}, {})
+    cotangent = follow(cotangent, (token_blocks[0], fetched[2]))
+    cot_blocks = spread(
+        cotangent, {layers - 1: fetched[0]}, {0: token_blocks[1], layers - 1: fetched[1]}
+    )
+
+    def in_order(blocks, start, size):
+        whole = jnp.zeros((layers * rows, size), blocks[0].dtype)
+        for step, block in enumerate(blocks):
+            at = (layer - step) % layers * rows
+            whole = lax.dynamic_update_slice(whole, block[:, start : start + size], (at, 0))
+        return whole
+
+    def cut(whole, step):
+        return lax.dynamic_slice(whole, ((layer - step) % layers * rows, 0), (rows, width))
+
+    token_sides = [in_order(blocks, 0, width) for blocks in token_blocks]
+    mark_sides = [in_order(blocks, width, experts) for blocks in token_blocks]
+    cot_sides = [in_order(blocks, 0, width) for blocks in cot_blocks]
+
+    both = jnp.concatenate(token_sides, axis=0)
+    logits = jnp.dot(both, router_weight, preferred_element_type=jnp.float32)
+    raised = jnp.where(jnp.concatenate(mark_sides, axis=0) > 0, jnp.exp(logits), 0.0)
+    probs = raised / jnp.sum(raised, axis=1, keepdims=True)
+    prob_sides = jnp.split(probs, 2, axis=0)
+
+    def expert_on(which, x, rows_in, after=None):
+        gate_mat, up_mat, down_mat = mats[which]
+        gate_act = jnp.dot(rows_in, gate_mat, preferred_element_type=jnp.float32)
+        up_act = jnp.dot(rows_in, up_mat, preferred_element_type=jnp.float32)
+        hidden = follow((jax.nn.silu(gate_act) * up_act).astype(jnp.bfloat16), after)
+        out = jnp.dot(hidden, down_mat, preferred_element_type=jnp.float32).astype(jnp.bfloat16)
+        out = out.astype(jnp.float32)
+        name = place * 2 + (copy if which == 0 else 1 - copy)
+        mine = jnp.sum(jnp.where(columns[None, :] == name, prob_sides[x], 0.0), axis=1, keepdims=True)
+        return mine * out, jnp.sum(out * cot_sides[x].astype(jnp.float32), axis=1)
+
+    own = [expert_on(0, x, follow(token_sides[x], fetched[2])) for x in range(2)]
+    other = [None, None]
+    other[1] = expert_on(1, 1, token_sides[1])
+    far = (own[1][0] + other[1][0]).astype(jnp.bfloat16)
+    first = [1, layers - 1]
+    rest = list(range(2, layers - 1)) + [0]
+    far_blocks = {step: cut(far, step) for step in first + rest}
+    held, far_blocks = lax.optimization_barrier((token_sides[0], far_blocks))
+    arrived = {step: swap(far_blocks[step]) for step in first}
+    other[0] = expert_on(1, 0, held, arrived[first[0]])
+    near = own[0][0] + other[0][0]
+
+    dots = jnp.stack([own[0][1], own[1][1], other[0][1], other[1][1]]).reshape(-1, 128)
+    dot_near = jnp.concatenate([dots] + [shift(dots, step) for step in range(1, layers)], axis=0)
+    dot_far = swap(dot_near)
+    held_far, dot_far = lax.optimization_barrier(([far_blocks[step] for step in rest], dot_far))
+    for step, block in zip(rest, held_far):
+        arrived[step] = swap(block)
+
+    mixed = None
+    for step in first + rest:
+        total = cut(near, step) + arrived[step].astype(jnp.float32)
+        if step:
+            total = shift(total.astype(jnp.bfloat16), -step).astype(jnp.float32)
+        mixed = total if mixed is None else mixed + total
+    mixed = mixed.astype(jnp.bfloat16)
+
+    table = jnp.zeros((2 * layers * rows, experts), jnp.float32)
+    for x, found in enumerate((dot_near, dot_far)):
+        found = found.reshape(layers, 2, 2, layers * rows)
+        if x:
+            found = jnp.flip(found, 2)
+        found = found.reshape(layers, 2, -1)
+        for step in range(layers):
+            there = ((layer - step) % layers * 2 + (side ^ x)) * 2
+            for which in range(2):
+                name = there + (copy if which == 0 else 1 - copy)
+                table = jnp.where(columns[None, :] == name, found[step, which][:, None], table)
+    grad_table = probs * (table - jnp.sum(probs * table, axis=1, keepdims=True))
+    pieces = lax.dot_general(
+        both.reshape(2, layers * rows, width),
+        split_three(grad_table).reshape(2, layers * rows, 3 * experts),
+        (((1,), (1,)), ((0,), (0,))),
+        preferred_element_type=jnp.float32,
+    )
+    grads = pieces[:, :, :experts] + pieces[:, :, experts : 2 * experts] + pieces[:, :, 2 * experts :]
+    grad = grads[0] + grads[1]
+    grad = grad + across(grad, "replica")
+    return mixed, grad + across(grad, "dp")
+
+
 def local(tokens, expert_ids, router_weight, gate_weight, up_weight, down_weight, cotangent):
     rows, width = tokens.shape
     experts = router_weight.shape[1]
+    if lax.axis_size("expert") == 8 and lax.axis_size("replica") == 2:
+        return paired(
+            tokens, expert_ids, router_weight, gate_weight, up_weight, down_weight, cotangent, 4
+        )
     chunks = max(1, experts // 16)
     mats = (gate_weight[0], up_weight[0], down_weight[0])
     if chunks == 1:

time: 829 us -> 563 us (0.68)
  waiting for transfers between devices: 657 us -> 299 us
  local copies, waits for them, and re-layouts: 0.08 us -> 86.8 us
  blocking collectives: 63 us -> 0 us
  starting transfers between devices: 0.18 us -> 36.1 us
  matrix products: 80.4 us -> 110 us
  between operations: 13.8 us -> 1.71 us
    reduce_scatter x1 -> x0, waiting for transfers between devices: 338 us -> none  [one_chunk(): mixed = lax.psum_scatter(part, GROUP, scatter_dimension=0, tiled=True)]
    all_gather x2 -> x0, waiting for transfers between devices: 316 us -> none  [the longest x1 162 us: one_chunk(): all_tokens = lax.all_gather(tokens, GROUP, axis=0, tiled=True)]
    ppermute x1 -> x33, waiting for transfers between devices: 1.52 us -> 299 us  [the longest x13 150 us: swap(): lax.ppermute(block, 'expert', [(e, e ^ 1) for e in range(2 * layers)])]
    all_gather x2 -> x0, blocking collectives: 63 us -> none  [the longest x1 32.2 us: one_chunk(): slot_dots = lax.all_gather(dots, GROUP, axis=0).T]
    ppermute x1 -> x33, starting transfers between devices: 0.07 us -> 36.1 us  [the longest x12 22.5 us: shift(): return lax.ppermute(block, 'expert', pairs)]
    dot_general x5 -> x11, matrix products: 80.4 us -> 110 us  [the longest x4 62.7 us: expert_on(): jnp.dot(hidden, down_mat, preferred_element_type=jnp.float32)]
    dynamic_update_slice x0 -> x24, local copies, waits for them, and re-layouts: none -> 26.6 us  [in_order(): lax.dynamic_update_slice(whole, block[:, start:start + size], (at, 0))]
    slice x0 -> x18, local copies, waits for them, and re-layouts: none -> 20.7 us  [the longest x16 20.7 us: in_order(): block[:, start:start + size]]
  transfers between devices with their start and end apart: 4 -> 33, of which waited for: 4 -> 20; matrix products, arithmetic and copies ran while one was open for 6% -> 31% of each run, Pallas kernels for 0% -> 0%
where the time goes in v3:
time: 563 us; the launch traced here: 552 us
  waiting for transfers between devices  299 us (53%)
  matrix products  110 us (20%)
  local copies, waits for them, and re-layouts  86.8 us (15%)
  starting transfers between devices  36.1 us (6%)
  other arithmetic  18.7 us (3%)
    ppermute x13, waiting for transfers between devices, swap(): lax.ppermute(block, 'expert', [(e, e ^ 1) for e in range(2 * layers)])  150 us
    ppermute x12, waiting for transfers between devices, shift(): return lax.ppermute(block, 'expert', pairs)  148 us
    dot_general x4, matrix products, expert_on(): jnp.dot(hidden, down_mat, preferred_element_type=jnp.float32)  62.7 us
    dynamic_update_slice x24, local copies, waits for them, and re-layouts, in_order(): lax.dynamic_update_slice(whole, block[:, start:start + size], (at, 0))  26.6 us
    dot_general x3, matrix products, expert_on(): up_act = jnp.dot(rows_in, up_mat, preferred_element_type=jnp.float32)  23 us
    ppermute x12, starting transfers between devices, shift(): return lax.ppermute(block, 'expert', pairs)  22.5 us
    slice x16, local copies, waits for them, and re-layouts, in_order(): block[:, start:start + size]  20.7 us
    dot_general x2, matrix products, expert_on(): gate_act = jnp.dot(rows_in, gate_mat, preferred_element_type=jnp.float32)  14.3 us
  transfers between devices with their start and end apart: 33, of which 20 were waited for; matrix products, arithmetic and copies ran while one was open for 31% of the time, Pallas kernels for 0%

profile of v3, /device:TPU:12, one launch (start us, length us, event | category | flops | bytes accessed | tf_op | source)
XLA Modules:
  0.0 552.1 jit_solution(15946541097346702063)
XLA Ops:
  35.1 45.7 %collective-permute-done = bf16[128,4224]{0,1:T(8,128)(2,1)} collective-permute-done((bf16[128,4224]{0,1:T(8,128)(2,1)S(1)}, bf16[128,4224]{0,1:T(8,128)(2,1)}, u32[]{:S(2)}, u32[]{:S(2)}) %collective-permute-start) | collective-permute-done | bytes 1081376 | tf_op jit(solution)/shard_map/ppermute | solution.py:59
  84.5 18.0 %collective-permute-done.1 = bf16[128,4224]{0,1:T(8,128)(2,1)} collective-permute-done((bf16[128,4224]{0,1:T(8,128)(2,1)S(1)}, bf16[128,4224]{0,1:T(8,128)(2,1)}, u32[]{:S(2)}, u32[]{:S(2)}) %collective-permute-start.1) | collective-permute-done | bytes 1081376 | tf_op jit(solution)/shard_map/ppermute | solution.py:59
  122.9 20.6 %collective-permute-done.4 = bf16[128,4224]{0,1:T(8,128)(2,1)S(1)} collective-permute-done((bf16[128,4224]{0,1:T(8,128)(2,1)}, bf16[128,4224]{0,1:T(8,128)(2,1)S(1)}, u32[]{:S(2)}, u32[]{:S(2)}) %collective-permute-start.4) | collective-permute-done | bytes 1081376 | tf_op jit(solution)/shard_map/ppermute | solution.py:62
  143.5 23.2 %collective-permute-done.5 = bf16[128,4224]{0,1:T(8,128)(2,1)S(1)} collective-permute-done((bf16[128,4224]{0,1:T(8,128)(2,1)}, bf16[128,4224]{0,1:T(8,128)(2,1)S(1)}, u32[]{:S(2)}, u32[]{:S(2)}) %collective-permute-start.5) | collective-permute-done | bytes 1081376 | tf_op jit(solution)/shard_map/ppermute | solution.py:62
  170.1 17.4 %collective-permute-done.6 = bf16[128,4224]{0,1:T(8,128)(2,1)} collective-permute-done((bf16[128,4224]{0,1:T(8,128)(2,1)}, bf16[128,4224]{0,1:T(8,128)(2,1)}, u32[]{:S(2)}, u32[]{:S(2)}) %collective-permute-start.6) | collective-permute-done | bytes 1081376 | tf_op jit(solution)/shard_map/ppermute | solution.py:62
  199.9 7.9 %pad_maximum_fusion = bf16[1024,4096]{1,0:T(8,128)(2,1)} fusion(bf16[512,4096]{1,0:T(8,128)(2,1)} %constant_dynamic-update-slice_fusion.18, bf16[512,4096]{1,0:T(8,128)(2,1)} %constant_dynamic-update-slice_fusion.22), kind=kLoop, calls=%fused_computation.15 | loop fusion | flops 16777216 | bytes 16777216 | tf_op jit(solution)/shard_map/concatenate | solution.py:113
  212.3 8.6 %fusion.11 = f32[512,768]{1,0:T(8,128)} fusion(bf16[512,4096]{1,0:T(8,128)(2,1)} %constant_dynamic-update-slice_fusion.18, bf16[1,4096,768]{2,1,0:T(8,128)(2,1)} %param.11), kind=kOutput, calls=%fused_computation.20 | convolution fusion | flops 3221225472 | bytes 12058624 | tf_op jit(solution)/shard_map/dot_general | solution.py:122
  220.9 17.2 %fusion.22 = bf16[512,4096]{1,0:T(8,128)(2,1)} fusion(bf16[1,768,4096]{2,1,0:T(8,128)(2,1)} %param.12, f32[512,768]{1,0:T(8,128)} %fusion.11, bf16[512,4096]{1,0:T(8,128)(2,1)} %constant_dynamic-update-slice_fusion.18, bf16[1,4096,768]{2,1,0:T(8,128)(2,1)} %param.10), kind=kOutput, calls=%fused_computation.29 | convolution fusion | flops 6446907392 | bytes 22544384 | tf_op jit(solution)/shard_map/dot_general | solution.py:124
  241.0 8.7 %fusion.13 = f32[512,768]{1,0:T(8,128)} fusion(bf16[512,4096]{1,0:T(8,128)(2,1)} %constant_dynamic-update-slice_fusion.22, bf16[1,4096,768]{2,1,0:T(8,128)(2,1)} %param.11), kind=kOutput, calls=%fused_computation.22 | convolution fusion | flops 3221225472 | bytes 12058624 | tf_op jit(solution)/shard_map/dot_general | solution.py:122
  249.7 17.2 %fusion.19 = bf16[512,4096]{1,0:T(8,128)(2,1)} fusion(bf16[1,768,4096]{2,1,0:T(8,128)(2,1)} %param.12, f32[512,768]{1,0:T(8,128)} %fusion.13, bf16[512,4096]{1,0:T(8,128)(2,1)} %constant_dynamic-update-slice_fusion.22, bf16[1,4096,768]{2,1,0:T(8,128)(2,1)} %param.10), kind=kOutput, calls=%fused_computation.28 | convolution fusion | flops 6446907392 | bytes 22544384 | tf_op jit(solution)/shard_map/dot_general | solution.py:124
  279.9 16.6 %collective-permute-done.18 = bf16[128,4096]{1,0:T(8,128)(2,1)} collective-permute-done((bf16[128,4096]{1,0:T(8,128)(2,1)}, bf16[128,4096]{1,0:T(8,128)(2,1)}, u32[]{:S(2)}, u32[]{:S(2)}) %collective-permute-start.18) | collective-permute-done | bytes 1048608 | tf_op jit(solution)/shard_map/ppermute | solution.py:59
  308.1 14.7 %collective-permute-done.21 = bf16[128,4096]{1,0:T(8,128)(2,1)S(1)} collective-permute-done((bf16[128,4096]{1,0:T(8,128)(2,1)}, bf16[128,4096]{1,0:T(8,128)(2,1)S(1)}, u32[]{:S(2)}, u32[]{:S(2)}) %collective-permute-start.21) | collective-permute-done | bytes 1048608 | tf_op jit(solution)/shard_map/ppermute | solution.py:62
  323.9 17.4 %collective-permute-done.22 = bf16[128,4096]{1,0:T(8,128)(2,1)S(1)} collective-permute-done((bf16[128,4096]{1,0:T(8,128)(2,1)}, bf16[128,4096]{1,0:T(8,128)(2,1)S(1)}, u32[]{:S(2)}, u32[]{:S(2)}) %collective-permute-start.22) | collective-permute-done | bytes 1048608 | tf_op jit(solution)/shard_map/ppermute | solution.py:62
  346.3 7.1 %fusion.52 = f32[512,768]{1,0:T(8,128)S(1)} fusion(bf16[512,4096]{1,0:T(8,128)(2,1)} %constant_dynamic-update-slice_fusion.18, bf16[4096,768]{1,0:T(8,128)(2,1)S(1)} %constant_dynamic-update-slice_fusion), kind=kOutput, calls=%fused_computation.137 | convolution fusion | flops 3221225472 | bytes 12058624 | tf_op jit(solution)/shard_map/dot_general | solution.py:121
  353.4 10.4 %collective-permute-done.23 = bf16[128,4096]{1,0:T(8,128)(2,1)S(1)} collective-permute-done((bf16[128,4096]{1,0:T(8,128)(2,1)}, bf16[128,4096]{1,0:T(8,128)(2,1)S(1)}, u32[]{:S(2)}, u32[]{:S(2)}) %collective-permute-start.23) | collective-permute-done | bytes 1048608 | tf_op jit(solution)/shard_map/ppermute | solution.py:62
  368.2 19.0 %fusion.5 = (f32[512]{0:T(512)S(1)}, f32[512]{0:T(512)S(1)}, bf16[512,4096]{1,0:T(8,128)(2,1)}) fusion(bf16[512,4096]{1,0:T(8,128)(2,1)} %constant_dynamic-update-slice_fusion.10, bf16[512,4096]{1,0:T(8,128)(2,1)} %fusion.22, f32[512]{0:T(512)S(1)} %get-tuple-element.44, f32[512]{0:T(512)S(1)} %get-tuple-element.41, bf16[768,4096]{1,0:T(8,128)(2,1)} %copy-done.4, ...), kind=kOutput, calls=%fused_computation.13 | convolution fusion | flops 6469975040 | bytes 30941184 | tf_op jit(solution)/shard_map/dot_general | solution.py:124
  390.9 7.2 %fusion.53 = f32[512,768]{1,0:T(8,128)S(1)} fusion(bf16[512,4096]{1,0:T(8,128)(2,1)} %constant_dynamic-update-slice_fusion.22, bf16[4096,768]{1,0:T(8,128)(2,1)} %copy-done.5), kind=kOutput, calls=%fused_computation.138 | convolution fusion | flops 3221225472 | bytes 12058624 | tf_op jit(solution)/shard_map/dot_general | solution.py:121
  400.2 5.7 %multiply_convert_fusion = bf16[512,768]{1,0:T(8,128)(2,1)S(1)} fusion(f32[512,768]{1,0:T(8,128)S(1)} %fusion.53, bf16[512,4096]{1,0:T(8,128)(2,1)} %constant_dynamic-update-slice_fusion.22, bf16[4096,768]{1,0:T(8,128)(2,1)S(1)} %bitcast.85), kind=kOutput, calls=%fused_computation.39 | convolution fusion | flops 3223584768 | bytes 12845056 | tf_op jit(solution)/shard_map/dot_general | solution.py:122
  405.9 18.4 %collective-permute-done.13 = bf16[128,4096]{1,0:T(8,128)(2,1)S(1)} collective-permute-done((bf16[128,4096]{1,0:T(8,128)(2,1)S(1)}, bf16[128,4096]{1,0:T(8,128)(2,1)S(1)}, u32[]{:S(2)}, u32[]{:S(2)}) %collective-permute-start.13) | collective-permute-done | bytes 1048608 | tf_op jit(solution)/shard_map/ppermute | solution.py:62
  424.4 9.3 %fusion.3 = (f32[512]{0:T(512)S(1)}, f32[512]{0:T(512)S(1)}, f32[512,4096]{1,0:T(8,128)}) fusion(bf16[512,4096]{1,0:T(8,128)(2,1)} %constant_dynamic-update-slice_fusion.14, bf16[512,4096]{1,0:T(8,128)(2,1)S(1)} %copy-done.24, f32[512]{0:T(512)S(1)} %get-tuple-element.45, f32[512]{0:T(512)S(1)} %get-tuple-element.40, ...), kind=kOutput, calls=%fused_computation.11 | convolution fusion | flops 3244293120 | bytes 23863296 | tf_op jit(solution)/shard_map/dot_general | solution.py:124
  446.7 5.1 fusion.37
  454.0 18.3 %collective-permute-done.28 = bf16[128,4096]{1,0:T(8,128)(2,1)S(1)} collective-permute-done((bf16[128,4096]{1,0:T(8,128)(2,1)S(1)}, bf16[128,4096]{1,0:T(8,128)(2,1)S(1)}, u32[]{:S(2)}, u32[]{:S(2)}) %collective-permute-start.28) | collective-permute-done | bytes 1048608 | tf_op jit(solution)/shard_map/ppermute | solution.py:62
  486.6 53.1 %collective-permute-done.14 = bf16[128,4096]{1,0:T(8,128)(2,1)S(1)} collective-permute-done((bf16[128,4096]{1,0:T(8,128)(2,1)S(1)}, bf16[128,4096]{1,0:T(8,128)(2,1)S(1)}, u32[]{:S(2)}, u32[]{:S(2)}) %collective-permute-start.14) | collective-permute-done | bytes 1048608 | tf_op jit(solution)/shard_map/ppermute | solution.py:59
  539.7 10.5 %collective-permute-done.29 = bf16[128,4096]{1,0:T(8,128)(2,1)S(1)} collective-permute-done((bf16[128,4096]{1,0:T(8,128)(2,1)S(1)}, bf16[128,4096]{1,0:T(8,128)(2,1)S(1)}, u32[]{:S(2)}, u32[]{:S(2)}) %collective-permute-start.29) | collective-permute-done | bytes 1048608 | tf_op jit(solution)/shard_map/ppermute | solution.py:59
  (212 shorter events, 153.3 us)
Async XLA Ops:
  8.5 72.2 %collective-permute-start = (bf16[128,4224]{0,1:T(8,128)(2,1)S(1)}, bf16[128,4224]{0,1:T(8,128)(2,1)}, u32[]{:S(2)}, u32[]{:S(2)}) collective-permute-start(bf16[128,4224]{0,1:T(8,128)(2,1)S(1)} %pad_maximum_fusion.1), channel_id=1, source_target_pairs={{0,4},{2,6},{4,8},{6,10},{8,12},{10,14},{12,0},{14,2},{1,5},{3,7},... | collective-permute-start | bytes 3244040 | tf_op jit(solution)/shard_map/ppermute | solution.py:59
  10.1 92.4 %collective-permute-start.1 = (bf16[128,4224]{0,1:T(8,128)(2,1)S(1)}, bf16[128,4224]{0,1:T(8,128)(2,1)}, u32[]{:S(2)}, u32[]{:S(2)}) collective-permute-start(bf16[128,4224]{0,1:T(8,128)(2,1)S(1)} %pad_maximum_fusion.1), channel_id=1, source_target_pairs={{0,8},{2,10},{4,12},{6,14},{8,0},{10,2},{12,4},{14,6},{1,9},{3,11}... | collective-permute-start | bytes 3244040 | tf_op jit(solution)/shard_map/ppermute | solution.py:59
  11.4 95.7 %collective-permute-start.2 = (bf16[128,4224]{0,1:T(8,128)(2,1)S(1)}, bf16[128,4224]{0,1:T(8,128)(2,1)}, u32[]{:S(2)}, u32[]{:S(2)}) collective-permute-start(bf16[128,4224]{0,1:T(8,128)(2,1)S(1)} %pad_maximum_fusion.1), channel_id=1, source_target_pairs={{0,12},{2,14},{4,0},{6,2},{8,4},{10,6},{12,8},{14,10},{1,13},{3,15... | collective-permute-start | bytes 3244040 | tf_op jit(solution)/shard_map/ppermute | solution.py:59
  13.2 194.7 %collective-permute-start.7 = (bf16[384,4096]{1,0:T(8,128)(2,1)}, bf16[384,4096]{1,0:T(8,128)(2,1)}, u32[]{:S(2)}, u32[]{:S(2)}) collective-permute-start(bf16[384,4096]{1,0:T(8,128)(2,1)} %dynamic-slice_bitcast_fusion.2), channel_id=1, source_target_pairs={{0,1},{1,0},{2,3},{3,2},{4,5},{5,4},{6,7},{7,6},{8,9},{9,8},{10,11... | collective-permute-start | bytes 9437192 | tf_op jit(solution)/shard_map/ppermute | solution.py:65
  32.8 205.4 %collective-permute-start.8 = (bf16[4096,384]{1,0:T(8,128)(2,1)}, bf16[4096,384]{1,0:T(8,128)(2,1)}, u32[]{:S(2)}, u32[]{:S(2)}) collective-permute-start(bf16[4096,384]{1,0:T(8,128)(2,1)} %dynamic-slice_bitcast_fusion.1), channel_id=1, source_target_pairs={{0,1},{1,0},{2,3},{3,2},{4,5},{5,4},{6,7},{7,6},{8,9},{9,8},{10,11... | collective-permute-start | bytes 9437192 | tf_op jit(solution)/shard_map/ppermute | solution.py:65
  116.5 27.0 %collective-permute-start.4 = (bf16[128,4224]{0,1:T(8,128)(2,1)}, bf16[128,4224]{0,1:T(8,128)(2,1)S(1)}, u32[]{:S(2)}, u32[]{:S(2)}) collective-permute-start(bf16[128,4224]{0,1:T(8,128)(2,1)} %collective-permute-done), channel_id=1, source_target_pairs={{0,2},{2,0},{4,6},{6,4},{8,10},{10,8},{12,14},{14,12},{1,3},{3,1},... | collective-permute-start | bytes 3244040 | tf_op jit(solution)/shard_map/ppermute | solution.py:62
  117.0 49.6 %collective-permute-start.5 = (bf16[128,4224]{0,1:T(8,128)(2,1)}, bf16[128,4224]{0,1:T(8,128)(2,1)S(1)}, u32[]{:S(2)}, u32[]{:S(2)}) collective-permute-start(bf16[128,4224]{0,1:T(8,128)(2,1)} %collective-permute-done.1), channel_id=1, source_target_pairs={{0,2},{2,0},{4,6},{6,4},{8,10},{10,8},{12,14},{14,12},{1,3},{3,1},... | collective-permute-start | bytes 3244040 | tf_op jit(solution)/shard_map/ppermute | solution.py:62
  118.5 69.0 %collective-permute-start.6 = (bf16[128,4224]{0,1:T(8,128)(2,1)}, bf16[128,4224]{0,1:T(8,128)(2,1)}, u32[]{:S(2)}, u32[]{:S(2)}) collective-permute-start(bf16[128,4224]{0,1:T(8,128)(2,1)} %collective-permute-done.2), channel_id=1, source_target_pairs={{0,2},{2,0},{4,6},{6,4},{8,10},{10,8},{12,14},{14,12},{1,3},{3,1},... | collective-permute-start | bytes 3244040 | tf_op jit(solution)/shard_map/ppermute | solution.py:62
  207.9 69.1 %collective-permute-start.17 = (bf16[128,4096]{1,0:T(8,128)(2,1)}, bf16[128,4096]{1,0:T(8,128)(2,1)}, u32[]{:S(2)}, u32[]{:S(2)}) collective-permute-start(bf16[128,4096]{1,0:T(8,128)(2,1)} %param.13), channel_id=1, source_target_pairs={{0,4},{2,6},{4,8},{6,10},{8,12},{10,14},{12,0},{14,2},{1,5},{3,7},... | collective-permute-start | bytes 3145736 | tf_op jit(solution)/shard_map/ppermute | solution.py:59
  208.2 88.3 %collective-permute-start.18 = (bf16[128,4096]{1,0:T(8,128)(2,1)}, bf16[128,4096]{1,0:T(8,128)(2,1)}, u32[]{:S(2)}, u32[]{:S(2)}) collective-permute-start(bf16[128,4096]{1,0:T(8,128)(2,1)} %param.13), channel_id=1, source_target_pairs={{0,8},{2,10},{4,12},{6,14},{8,0},{10,2},{12,4},{14,6},{1,9},{3,11}... | collective-permute-start | bytes 3145736 | tf_op jit(solution)/shard_map/ppermute | solution.py:59
  211.8 67.6 %collective-permute-start.20 = (bf16[128,4096]{1,0:T(8,128)(2,1)}, bf16[128,4096]{1,0:T(8,128)(2,1)}, u32[]{:S(2)}, u32[]{:S(2)}) collective-permute-start(bf16[128,4096]{1,0:T(8,128)(2,1)} %param.13), channel_id=1, source_target_pairs={{0,2},{2,0},{4,6},{6,4},{8,10},{10,8},{12,14},{14,12},{1,3},{3,1},... | collective-permute-start | bytes 3145736 | tf_op jit(solution)/shard_map/ppermute | solution.py:62
  238.1 62.4 %collective-permute-start.19 = (bf16[128,4096]{1,0:T(8,128)(2,1)}, bf16[128,4096]{1,0:T(8,128)(2,1)}, u32[]{:S(2)}, u32[]{:S(2)}) collective-permute-start(bf16[128,4096]{1,0:T(8,128)(2,1)} %param.13), channel_id=1, source_target_pairs={{0,12},{2,14},{4,0},{6,2},{8,4},{10,6},{12,8},{14,10},{1,13},{3,15... | collective-permute-start | bytes 3145736 | tf_op jit(solution)/shard_map/ppermute | solution.py:59
  240.5 83.4 %collective-permute-start.10 = (bf16[4096,384]{1,0:T(8,128)(2,1)S(1)}, bf16[4096,384]{1,0:T(8,128)(2,1)}, u32[]{:S(2)}, u32[]{:S(2)}) collective-permute-start(bf16[4096,384]{1,0:T(8,128)(2,1)S(1)} %copy-done.3), channel_id=1, source_target_pairs={{0,1},{1,0},{2,3},{3,2},{4,5},{5,4},{6,7},{7,6},{8,9},{9,8},{10,11... | collective-permute-start | bytes 9437192 | tf_op jit(solution)/shard_map/ppermute | solution.py:65
  277.0 68.1 %collective-permute-start.9 = (bf16[4096,384]{1,0:T(8,128)(2,1)}, bf16[4096,384]{1,0:T(8,128)(2,1)S(1)}, u32[]{:S(2)}, u32[]{:S(2)}) collective-permute-start(bf16[4096,384]{1,0:T(8,128)(2,1)} %collective-permute-done.8), channel_id=1, source_target_pairs={{0,16},{16,0},{1,17},{17,1},{2,18},{18,2},{3,19},{19,3},{4,20},{20... | collective-permute-start | bytes 9437192 | tf_op jit(solution)/shard_map/ppermute | solution.py:65
  279.4 66.4 %collective-permute-start.12 = (bf16[384,4096]{1,0:T(8,128)(2,1)}, bf16[384,4096]{1,0:T(8,128)(2,1)S(1)}, u32[]{:S(2)}, u32[]{:S(2)}) collective-permute-start(bf16[384,4096]{1,0:T(8,128)(2,1)} %collective-permute-done.7), channel_id=1, source_target_pairs={{0,16},{16,0},{1,17},{17,1},{2,18},{18,2},{3,19},{19,3},{4,20},{20... | collective-permute-start | bytes 9437192 | tf_op jit(solution)/shard_map/ppermute | solution.py:65
  296.5 26.3 %collective-permute-start.21 = (bf16[128,4096]{1,0:T(8,128)(2,1)}, bf16[128,4096]{1,0:T(8,128)(2,1)S(1)}, u32[]{:S(2)}, u32[]{:S(2)}) collective-permute-start(bf16[128,4096]{1,0:T(8,128)(2,1)} %collective-permute-done.17), channel_id=1, source_target_pairs={{0,2},{2,0},{4,6},{6,4},{8,10},{10,8},{12,14},{14,12},{1,3},{3,1},... | collective-permute-start | bytes 3145736 | tf_op jit(solution)/shard_map/ppermute | solution.py:62
  300.5 40.8 %collective-permute-start.22 = (bf16[128,4096]{1,0:T(8,128)(2,1)}, bf16[128,4096]{1,0:T(8,128)(2,1)S(1)}, u32[]{:S(2)}, u32[]{:S(2)}) collective-permute-start(bf16[128,4096]{1,0:T(8,128)(2,1)} %collective-permute-done.18), channel_id=1, source_target_pairs={{0,2},{2,0},{4,6},{6,4},{8,10},{10,8},{12,14},{14,12},{1,3},{3,1},... | collective-permute-start | bytes 3145736 | tf_op jit(solution)/shard_map/ppermute | solution.py:62
  323.9 41.0 %collective-permute-start.11 = (bf16[4096,384]{1,0:T(8,128)(2,1)}, bf16[4096,384]{1,0:T(8,128)(2,1)S(1)}, u32[]{:S(2)}, u32[]{:S(2)}) collective-permute-start(bf16[4096,384]{1,0:T(8,128)(2,1)} %collective-permute-done.10), channel_id=1, source_target_pairs={{0,16},{16,0},{1,17},{17,1},{2,18},{18,2},{3,19},{19,3},{4,20},{20... | collective-permute-start | bytes 9437192 | tf_op jit(solution)/shard_map/ppermute | solution.py:65
  398.7 55.3 %collective-permute-start.15 = (bf16[128,4096]{1,0:T(8,128)(2,1)}, bf16[128,4096]{1,0:T(8,128)(2,1)}, u32[]{:S(2)}, u32[]{:S(2)}) collective-permute-start(bf16[128,4096]{1,0:T(8,128)(2,1)} %get-tuple-element.26), channel_id=1, source_target_pairs={{0,2},{2,0},{4,6},{6,4},{8,10},{10,8},{12,14},{14,12},{1,3},{3,1},... | collective-permute-start | bytes 3145736 | tf_op jit(solution)/shard_map/ppermute | solution.py:62
  451.9 28.9 %collective-permute-start.31 = (f32[4096,16]{0,1:T(8,128)S(1)}, f32[4096,16]{0,1:T(8,128)S(1)}, u32[]{:S(2)}, u32[]{:S(2)}) collective-permute-start(f32[4096,16]{0,1:T(8,128)S(1)} %fusion.36), channel_id=1, source_target_pairs={{0,1},{1,0},{2,3},{3,2},{4,5},{5,4},{6,7},{7,6},{8,9},{9,8},{10,11... | collective-permute-start | bytes 786440 | tf_op jit(solution)/shard_map/ppermute | solution.py:65
  452.5 34.1 %collective-permute-start.30 = (bf16[128,4096]{1,0:T(8,128)(2,1)S(1)}, bf16[128,4096]{1,0:T(8,128)(2,1)S(1)}, u32[]{:S(2)}, u32[]{:S(2)}) collective-permute-start(bf16[128,4096]{1,0:T(8,128)(2,1)S(1)} %get-tuple-element.34), channel_id=1, source_target_pairs={{0,2},{2,0},{4,6},{6,4},{8,10},{10,8},{12,14},{14,12},{1,3},{3,1},... | collective-permute-start | bytes 3145736 | tf_op jit(solution)/shard_map/ppermute | solution.py:62
  474.5 65.2 %collective-permute-start.14 = (bf16[128,4096]{1,0:T(8,128)(2,1)S(1)}, bf16[128,4096]{1,0:T(8,128)(2,1)S(1)}, u32[]{:S(2)}, u32[]{:S(2)}) collective-permute-start(bf16[128,4096]{1,0:T(8,128)(2,1)S(1)} %get-tuple-element.48), channel_id=1, source_target_pairs={{0,12},{2,14},{4,0},{6,2},{8,4},{10,6},{12,8},{14,10},{1,13},{3,15... | collective-permute-start | bytes 3145736 | tf_op jit(solution)/shard_map/ppermute | solution.py:59
  474.6 65.1 %collective-permute-start.16 = (bf16[128,4096]{1,0:T(8,128)(2,1)S(1)}, bf16[128,4096]{1,0:T(8,128)(2,1)S(1)}, u32[]{:S(2)}, u32[]{:S(2)}) collective-permute-start(bf16[128,4096]{1,0:T(8,128)(2,1)S(1)} %get-tuple-element.50), channel_id=1, source_target_pairs={{0,4},{2,6},{4,8},{6,10},{8,12},{10,14},{12,0},{14,2},{1,5},{3,7},... | collective-permute-start | bytes 3145736 | tf_op jit(solution)/shard_map/ppermute | solution.py:59
  476.6 73.5 %collective-permute-start.29 = (bf16[128,4096]{1,0:T(8,128)(2,1)S(1)}, bf16[128,4096]{1,0:T(8,128)(2,1)S(1)}, u32[]{:S(2)}, u32[]{:S(2)}) collective-permute-start(bf16[128,4096]{1,0:T(8,128)(2,1)S(1)} %get-tuple-element.49), channel_id=1, source_target_pairs={{0,8},{2,10},{4,12},{6,14},{8,0},{10,2},{12,4},{14,6},{1,9},{3,11}... | collective-permute-start | bytes 3145736 | tf_op jit(solution)/shard_map/ppermute | solution.py:59
  (40 other events, 936.1 us)

commit v4 on v3

--- a/solution.py
+++ b/solution.py
@@ -67,9 +67,13 @@
     def follow(block, after):
         return block if after is None else lax.optimization_barrier((block, after))[0]
 
-    def spread(block, shifts, swaps):
+    def spread(block, shifts, start, last=None):
         near = [block] + [shift(follow(block, shifts.get(step)), step) for step in range(1, layers)]
-        return [near, [swap(follow(one, swaps.get(step))) for step, one in enumerate(near)]]
+        far = []
+        for step, one in enumerate(near):
+            after = [far[step - 2] if step >= 2 else start, last if step == layers - 1 else None]
+            far.append(swap(follow(one, [one for one in after if one is not None])))
+        return [near, far]
 
     first_half = core * half
     sent = (
@@ -77,9 +81,10 @@
         lax.dynamic_slice(up_weight[0], (0, first_half), (width, half)),
         lax.dynamic_slice(down_weight[0], (first_half, 0), (half, width)),
     )
-    fetched = [across(sent[0], "replica"), None, across(sent[2], "replica")]
-    later, _ = lax.optimization_barrier((sent[1], fetched[2]))
-    fetched[1] = across(later, "replica")
+    fetched = {2: across(sent[2], "replica")}
+    fetched[0] = across(sent[0], "replica")
+    fetched[1] = across(follow(sent[1], fetched[2]), "replica")
+    fetched = [fetched[which] for which in range(3)]
     second = [
         jnp.concatenate([part, across(part, "dp")], axis=axis) for part, axis in zip(fetched, (1, 1, 0))
     ]
@@ -90,11 +95,10 @@
     marks = jnp.pad(chosen.astype(jnp.bfloat16), ((0, 0), (0, -experts % 128)))
     marked = jnp.concatenate([tokens, marks], axis=1)
     marked, _ = lax.optimization_barrier((marked, sent[2]))
-    token_blocks = spread(marked, {}, {})
+    token_blocks = spread(marked, {}, None, fetched[2])
     cotangent = follow(cotangent, (token_blocks[0], fetched[2]))
-    cot_blocks = spread(
-        cotangent, {layers - 1: fetched[0]}, {0: token_blocks[1], layers - 1: fetched[1]}
-    )
+    cot_blocks = spread(cotangent, {layers - 1: fetched[0]}, token_blocks[1][layers - 1])
+    cot_blocks[1][layers - 1] = follow(cot_blocks[1][layers - 1], fetched[1])
 
     def in_order(blocks, start, size):
         whole = jnp.zeros((layers * rows, size), blocks[0].dtype)
@@ -131,8 +135,8 @@
     other = [None, None]
     other[1] = expert_on(1, 1, token_sides[1])
     far = (own[1][0] + other[1][0]).astype(jnp.bfloat16)
-    first = [1, layers - 1]
-    rest = list(range(2, layers - 1)) + [0]
+    first = [2, 1]
+    rest = [3, 0]
     far_blocks = {step: cut(far, step) for step in first + rest}
     held, far_blocks = lax.optimization_barrier((token_sides[0], far_blocks))
     arrived = {step: swap(far_blocks[step]) for step in first}
@@ -146,11 +150,12 @@
     for step, block in zip(rest, held_far):
         arrived[step] = swap(block)
 
-    mixed = None
+    mixed, before = None, None
     for step in first + rest:
-        total = cut(near, step) + arrived[step].astype(jnp.float32)
+        total = cut(near, step) + follow(arrived[step], before).astype(jnp.float32)
         if step:
-            total = shift(total.astype(jnp.bfloat16), -step).astype(jnp.float32)
+            before = total.astype(jnp.bfloat16)
+            total = shift(before, -step).astype(jnp.float32)
         mixed = total if mixed is None else mixed + total
     mixed = mixed.astype(jnp.bfloat16)
 

time: 563 us -> 520 us (0.924)
  waiting for transfers between devices: 299 us -> 257 us
    ppermute x13, waiting for transfers between devices: 150 us -> 111 us  [swap(): lax.ppermute(block, 'expert', [(e, e ^ 1) for e in range(2 * layers)])]
    ppermute x12, waiting for transfers between devices: 148 us -> 133 us  [shift(): return lax.ppermute(block, 'expert', pairs)]
    ppermute x8, waiting for transfers between devices: 1.54 us -> 13.1 us  [across(): return lax.ppermute(block, axis, [(0, 1), (1, 0)])]
    ppermute x12, starting transfers between devices: 22.5 us -> 15 us  [shift(): return lax.ppermute(block, 'expert', pairs)]
    unnamed x69 -> x83, local copies, waits for them, and re-layouts: 12.1 us -> 18.9 us
    ppermute x13, starting transfers between devices: 10.9 us -> 16.7 us  [swap(): lax.ppermute(block, 'expert', [(e, e ^ 1) for e in range(2 * layers)])]
  transfers between devices with their start and end apart: 33 -> 33, of which waited for: 20 -> 19; matrix products, arithmetic and copies ran while one was open for 31% -> 34% of each run, Pallas kernels for 0% -> 0%
where the time goes in v4:
time: 520 us; the launch traced here: 514 us
  waiting for transfers between devices  257 us (49%)
  matrix products  108 us (21%)
  local copies, waits for them, and re-layouts  89.1 us (17%)
  starting transfers between devices  34.9 us (7%)
  other arithmetic  23.5 us (5%)
    ppermute x12, waiting for transfers between devices, shift(): return lax.ppermute(block, 'expert', pairs)  133 us
    ppermute x13, waiting for transfers between devices, swap(): lax.ppermute(block, 'expert', [(e, e ^ 1) for e in range(2 * layers)])  111 us
    dot_general x4, matrix products, expert_on(): jnp.dot(hidden, down_mat, preferred_element_type=jnp.float32)  60.4 us
    dynamic_update_slice x24, local copies, waits for them, and re-layouts, in_order(): lax.dynamic_update_slice(whole, block[:, start:start + size], (at, 0))  22 us
    dot_general x3, matrix products, expert_on(): up_act = jnp.dot(rows_in, up_mat, preferred_element_type=jnp.float32)  21.7 us
    unnamed x83, local copies, waits for them, and re-layouts  18.9 us
    slice x16, local copies, waits for them, and re-layouts, in_order(): block[:, start:start + size]  17.7 us
    ppermute x13, starting transfers between devices, swap(): lax.ppermute(block, 'expert', [(e, e ^ 1) for e in range(2 * layers)])  16.7 us
  transfers between devices with their start and end apart: 33, of which 19 were waited for; matrix products, arithmetic and copies ran while one was open for 34% of the time, Pallas kernels for 0%

profile of v4, /device:TPU:12, one launch (start us, length us, event | category | flops | bytes accessed | tf_op | source)
XLA Modules:
  0.0 514.5 jit_solution(13475601715650063058)
XLA Ops:
  30.3 6.6 %collective-permute-done.3 = bf16[128,4224]{0,1:T(8,128)(2,1)} collective-permute-done((bf16[128,4224]{0,1:T(8,128)(2,1)S(1)}, bf16[128,4224]{0,1:T(8,128)(2,1)}, u32[]{:S(2)}, u32[]{:S(2)}) %collective-permute-start.3) | collective-permute-done | bytes 1081376 | tf_op jit(solution)/shard_map/ppermute | solution.py:62
  40.2 39.1 %collective-permute-done = bf16[128,4224]{0,1:T(8,128)(2,1)} collective-permute-done((bf16[128,4224]{0,1:T(8,128)(2,1)S(1)}, bf16[128,4224]{0,1:T(8,128)(2,1)}, u32[]{:S(2)}, u32[]{:S(2)}) %collective-permute-start) | collective-permute-done | bytes 1081376 | tf_op jit(solution)/shard_map/ppermute | solution.py:59
  80.8 20.5 %collective-permute-done.1 = bf16[128,4224]{0,1:T(8,128)(2,1)} collective-permute-done((bf16[128,4224]{0,1:T(8,128)(2,1)S(1)}, bf16[128,4224]{0,1:T(8,128)(2,1)}, u32[]{:S(2)}, u32[]{:S(2)}) %collective-permute-start.1) | collective-permute-done | bytes 1081376 | tf_op jit(solution)/shard_map/ppermute | solution.py:59
  136.9 11.6 %collective-permute-done.8 = bf16[4096,384]{1,0:T(8,128)(2,1)} collective-permute-done((bf16[4096,384]{1,0:T(8,128)(2,1)}, bf16[4096,384]{1,0:T(8,128)(2,1)}, u32[]{:S(2)}, u32[]{:S(2)}) %collective-permute-start.8) | collective-permute-done | bytes 3145760 | tf_op jit(solution)/shard_map/ppermute | solution.py:65
  150.6 8.6 %fusion.13 = f32[512,768]{1,0:T(8,128)} fusion(bf16[512,4096]{1,0:T(8,128)(2,1)} %constant_dynamic-update-slice_fusion.22, bf16[1,4096,768]{2,1,0:T(8,128)(2,1)} %param.11), kind=kOutput, calls=%fused_computation.22 | convolution fusion | flops 3221225472 | bytes 12058624 | tf_op jit(solution)/shard_map/dot_general | solution.py:126
  159.3 17.1 %fusion.19 = bf16[512,4096]{1,0:T(8,128)(2,1)} fusion(bf16[1,768,4096]{2,1,0:T(8,128)(2,1)} %param.12, f32[512,768]{1,0:T(8,128)} %fusion.13, bf16[512,4096]{1,0:T(8,128)(2,1)} %constant_dynamic-update-slice_fusion.22, bf16[1,4096,768]{2,1,0:T(8,128)(2,1)} %param.10), kind=kOutput, calls=%fused_computation.28 | convolution fusion | flops 6446907392 | bytes 22544384 | tf_op jit(solution)/shard_map/dot_general | solution.py:128
  184.9 15.5 %collective-permute-done.17 = bf16[128,4096]{1,0:T(8,128)(2,1)} collective-permute-done((bf16[128,4096]{1,0:T(8,128)(2,1)S(1)}, bf16[128,4096]{1,0:T(8,128)(2,1)}, u32[]{:S(2)}, u32[]{:S(2)}) %collective-permute-start.17) | collective-permute-done | bytes 1048608 | tf_op jit(solution)/shard_map/ppermute | solution.py:59
  201.7 18.4 %collective-permute-done.18 = bf16[128,4096]{1,0:T(8,128)(2,1)S(1)} collective-permute-done((bf16[128,4096]{1,0:T(8,128)(2,1)S(1)}, bf16[128,4096]{1,0:T(8,128)(2,1)S(1)}, u32[]{:S(2)}, u32[]{:S(2)}) %collective-permute-start.18) | collective-permute-done | bytes 1048608 | tf_op jit(solution)/shard_map/ppermute | solution.py:59
  230.6 7.0 %fusion.11 = f32[512,768]{1,0:T(8,128)S(1)} fusion(bf16[512,4096]{1,0:T(8,128)(2,1)} %constant_dynamic-update-slice_fusion.18, bf16[1,4096,768]{2,1,0:T(8,128)(2,1)} %param.11), kind=kOutput, calls=%fused_computation.20 | convolution fusion | flops 3221225472 | bytes 12058624 | tf_op jit(solution)/shard_map/dot_general | solution.py:126
  237.6 16.7 %fusion.22 = bf16[512,4096]{1,0:T(8,128)(2,1)} fusion(bf16[1,768,4096]{2,1,0:T(8,128)(2,1)} %param.12, f32[512,768]{1,0:T(8,128)S(1)} %fusion.11, bf16[512,4096]{1,0:T(8,128)(2,1)} %constant_dynamic-update-slice_fusion.18, bf16[1,4096,768]{2,1,0:T(8,128)(2,1)} %param.10), kind=kOutput, calls=%fused_computation.29 | convolution fusion | flops 6446907392 | bytes 22544384 | tf_op jit(solution)/shard_map/dot_general | solution.py:128
  262.1 8.0 %pad_maximum_fusion = bf16[1024,4096]{1,0:T(8,128)(2,1)} fusion(bf16[512,4096]{1,0:T(8,128)(2,1)} %constant_dynamic-update-slice_fusion.18, bf16[512,4096]{1,0:T(8,128)(2,1)} %constant_dynamic-update-slice_fusion.22), kind=kLoop, calls=%fused_computation.15 | loop fusion | flops 16777216 | bytes 16777216 | tf_op jit(solution)/shard_map/concatenate | solution.py:117
  270.1 10.4 %collective-permute-done.20 = bf16[128,4096]{1,0:T(8,128)(2,1)} collective-permute-done((bf16[128,4096]{1,0:T(8,128)(2,1)S(1)}, bf16[128,4096]{1,0:T(8,128)(2,1)}, u32[]{:S(2)}, u32[]{:S(2)}) %collective-permute-start.20) | collective-permute-done | bytes 1048608 | tf_op jit(solution)/shard_map/ppermute | solution.py:62
  281.9 21.0 %collective-permute-done.21 = bf16[128,4096]{1,0:T(8,128)(2,1)} collective-permute-done((bf16[128,4096]{1,0:T(8,128)(2,1)}, bf16[128,4096]{1,0:T(8,128)(2,1)}, u32[]{:S(2)}, u32[]{:S(2)}) %collective-permute-start.21) | collective-permute-done | bytes 1048608 | tf_op jit(solution)/shard_map/ppermute | solution.py:62
  321.6 9.1 %fusion.52 = f32[512,768]{1,0:T(8,128)} fusion(bf16[512,4096]{1,0:T(8,128)(2,1)} %constant_dynamic-update-slice_fusion.18, bf16[4096,768]{1,0:T(8,128)(2,1)S(1)} %copy-done.5), kind=kOutput, calls=%fused_computation.137 | convolution fusion | flops 3221225472 | bytes 12058624 | tf_op jit(solution)/shard_map/dot_general | solution.py:125
  330.7 16.1 %collective-permute-done.23 = bf16[128,4096]{1,0:T(8,128)(2,1)S(1)} collective-permute-done((bf16[128,4096]{1,0:T(8,128)(2,1)S(1)}, bf16[128,4096]{1,0:T(8,128)(2,1)S(1)}, u32[]{:S(2)}, u32[]{:S(2)}) %collective-permute-start.23) | collective-permute-done | bytes 1048608 | tf_op jit(solution)/shard_map/ppermute | solution.py:62
  352.4 19.0 %fusion.5 = (f32[512]{0:T(512)S(1)}, f32[512]{0:T(512)S(1)}, bf16[512,4096]{1,0:T(8,128)(2,1)}) fusion(bf16[512,4096]{1,0:T(8,128)(2,1)} %constant_dynamic-update-slice_fusion.10, bf16[512,4096]{1,0:T(8,128)(2,1)} %fusion.22, f32[512]{0:T(512)S(1)} %get-tuple-element.60, f32[512]{0:T(512)S(1)} %get-tuple-element.57, bf16[768,4096]{1,0:T(8,128)(2,1)} %copy-done.4, ...), kind=kOutput, calls=%fused_computation.13 | convolution fusion | flops 6469975040 | bytes 30941184 | tf_op jit(solution)/shard_map/dot_general | solution.py:128
  375.1 7.4 %fusion.53 = f32[512,768]{1,0:T(8,128)S(1)} fusion(bf16[512,4096]{1,0:T(8,128)(2,1)} %constant_dynamic-update-slice_fusion.22, bf16[4096,768]{1,0:T(8,128)(2,1)} %constant_dynamic-update-slice_fusion), kind=kOutput, calls=%fused_computation.138 | convolution fusion | flops 3221225472 | bytes 12058624 | tf_op jit(solution)/shard_map/dot_general | solution.py:125
  384.6 6.0 %multiply_convert_fusion = bf16[512,768]{1,0:T(8,128)(2,1)S(1)} fusion(f32[512,768]{1,0:T(8,128)S(1)} %fusion.53, bf16[512,4096]{1,0:T(8,128)(2,1)} %constant_dynamic-update-slice_fusion.22, bf16[4096,768]{1,0:T(8,128)(2,1)S(1)} %bitcast.87), kind=kOutput, calls=%fused_computation.39 | convolution fusion | flops 3223584768 | bytes 12845056 | tf_op jit(solution)/shard_map/dot_general | solution.py:126
  390.6 18.2 %collective-permute-done.13 = bf16[128,4096]{1,0:T(8,128)(2,1)} collective-permute-done((bf16[128,4096]{1,0:T(8,128)(2,1)S(1)}, bf16[128,4096]{1,0:T(8,128)(2,1)}, u32[]{:S(2)}, u32[]{:S(2)}) %collective-permute-start.13) | collective-permute-done | bytes 1048608 | tf_op jit(solution)/shard_map/ppermute | solution.py:62
  408.8 7.5 %fusion.3 = (f32[512]{0:T(512)S(1)}, f32[512]{0:T(512)S(1)}, f32[512,4096]{1,0:T(8,128)}) fusion(bf16[512,4096]{1,0:T(8,128)(2,1)S(1)} %copy-done.3, bf16[512,4096]{1,0:T(8,128)(2,1)S(1)} %copy-done.28, f32[512]{0:T(512)S(1)} %get-tuple-element.61, f32[512]{0:T(512)S(1)} %get-tuple-element.56, bf16[512,768]{1,0:T(8,128)(2,1)S(1)} %multiply_convert_fusion, ...), kind=kOutput, calls=%fused_computation.11 | convolution fusion | flops 3244293120 | bytes 23863296 | tf_op jit(solution)/shard_map/dot_general | solution.py:128
  432.5 7.0 %collective-permute-done.26 = f32[16,128]{1,0:T(8,128)S(1)} collective-permute-done((f32[16,128]{1,0:T(8,128)S(1)}, f32[16,128]{1,0:T(8,128)S(1)}, u32[]{:S(2)}, u32[]{:S(2)}) %collective-permute-start.26) | collective-permute-done | bytes 8224 | tf_op jit(solution)/shard_map/ppermute | solution.py:59
  452.8 18.0 %collective-permute-done.28 = bf16[128,4096]{1,0:T(8,128)(2,1)S(1)} collective-permute-done((bf16[128,4096]{1,0:T(8,128)(2,1)S(1)}, bf16[128,4096]{1,0:T(8,128)(2,1)S(1)}, u32[]{:S(2)}, u32[]{:S(2)}) %collective-permute-start.28) | collective-permute-done | bytes 1048608 | tf_op jit(solution)/shard_map/ppermute | solution.py:62
  473.5 9.2 %collective-permute-done.30 = bf16[128,4096]{1,0:T(8,128)(2,1)S(1)} collective-permute-done((bf16[128,4096]{1,0:T(8,128)(2,1)S(1)}, bf16[128,4096]{1,0:T(8,128)(2,1)S(1)}, u32[]{:S(2)}, u32[]{:S(2)}) %collective-permute-start.30) | collective-permute-done | bytes 1048608 | tf_op jit(solution)/shard_map/ppermute | solution.py:62
  482.7 28.3 %collective-permute-done.16 = bf16[128,4096]{1,0:T(8,128)(2,1)} collective-permute-done((bf16[128,4096]{1,0:T(8,128)(2,1)}, bf16[128,4096]{1,0:T(8,128)(2,1)}, u32[]{:S(2)}, u32[]{:S(2)}) %collective-permute-start.16) | collective-permute-done | bytes 1048608 | tf_op jit(solution)/shard_map/ppermute | solution.py:59
  (229 shorter events, 166.4 us)
Async XLA Ops:
  7.1 72.2 %collective-permute-start = (bf16[128,4224]{0,1:T(8,128)(2,1)S(1)}, bf16[128,4224]{0,1:T(8,128)(2,1)}, u32[]{:S(2)}, u32[]{:S(2)}) collective-permute-start(bf16[128,4224]{0,1:T(8,128)(2,1)S(1)} %pad_maximum_fusion.1), channel_id=1, source_target_pairs={{0,4},{2,6},{4,8},{6,10},{8,12},{10,14},{12,0},{14,2},{1,5},{3,7},... | collective-permute-start | bytes 3244040 | tf_op jit(solution)/shard_map/ppermute | solution.py:59
  8.7 92.6 %collective-permute-start.1 = (bf16[128,4224]{0,1:T(8,128)(2,1)S(1)}, bf16[128,4224]{0,1:T(8,128)(2,1)}, u32[]{:S(2)}, u32[]{:S(2)}) collective-permute-start(bf16[128,4224]{0,1:T(8,128)(2,1)S(1)} %pad_maximum_fusion.1), channel_id=1, source_target_pairs={{0,8},{2,10},{4,12},{6,14},{8,0},{10,2},{12,4},{14,6},{1,9},{3,11}... | collective-permute-start | bytes 3244040 | tf_op jit(solution)/shard_map/ppermute | solution.py:59
  10.0 104.1 %collective-permute-start.2 = (bf16[128,4224]{0,1:T(8,128)(2,1)S(1)}, bf16[128,4224]{0,1:T(8,128)(2,1)}, u32[]{:S(2)}, u32[]{:S(2)}) collective-permute-start(bf16[128,4224]{0,1:T(8,128)(2,1)S(1)} %pad_maximum_fusion.1), channel_id=1, source_target_pairs={{0,12},{2,14},{4,0},{6,2},{8,4},{10,6},{12,8},{14,10},{1,13},{3,15... | collective-permute-start | bytes 3244040 | tf_op jit(solution)/shard_map/ppermute | solution.py:59
  11.8 120.1 %collective-permute-start.6 = (bf16[384,4096]{1,0:T(8,128)(2,1)}, bf16[384,4096]{1,0:T(8,128)(2,1)}, u32[]{:S(2)}, u32[]{:S(2)}) collective-permute-start(bf16[384,4096]{1,0:T(8,128)(2,1)} %dynamic-slice_bitcast_fusion.2), channel_id=1, source_target_pairs={{0,1},{1,0},{2,3},{3,2},{4,5},{5,4},{6,7},{7,6},{8,9},{9,8},{10,11... | collective-permute-start | bytes 9437192 | tf_op jit(solution)/shard_map/ppermute | solution.py:65
  36.9 111.6 %collective-permute-start.8 = (bf16[4096,384]{1,0:T(8,128)(2,1)}, bf16[4096,384]{1,0:T(8,128)(2,1)}, u32[]{:S(2)}, u32[]{:S(2)}) collective-permute-start(bf16[4096,384]{1,0:T(8,128)(2,1)} %dynamic-slice_bitcast_fusion.1), channel_id=1, source_target_pairs={{0,1},{1,0},{2,3},{3,2},{4,5},{5,4},{6,7},{7,6},{8,9},{9,8},{10,11... | collective-permute-start | bytes 9437192 | tf_op jit(solution)/shard_map/ppermute | solution.py:65
  79.3 42.4 %collective-permute-start.4 = (bf16[128,4224]{0,1:T(8,128)(2,1)}, bf16[128,4224]{0,1:T(8,128)(2,1)}, u32[]{:S(2)}, u32[]{:S(2)}) collective-permute-start(bf16[128,4224]{0,1:T(8,128)(2,1)} %collective-permute-done), channel_id=1, source_target_pairs={{0,2},{2,0},{4,6},{6,4},{8,10},{10,8},{12,14},{14,12},{1,3},{3,1},... | collective-permute-start | bytes 3244040 | tf_op jit(solution)/shard_map/ppermute | solution.py:62
  131.8 68.6 %collective-permute-start.17 = (bf16[128,4096]{1,0:T(8,128)(2,1)S(1)}, bf16[128,4096]{1,0:T(8,128)(2,1)}, u32[]{:S(2)}, u32[]{:S(2)}) collective-permute-start(bf16[128,4096]{1,0:T(8,128)(2,1)S(1)} %copy-done.7), channel_id=1, source_target_pairs={{0,4},{2,6},{4,8},{6,10},{8,12},{10,14},{12,0},{14,2},{1,5},{3,7},... | collective-permute-start | bytes 3145736 | tf_op jit(solution)/shard_map/ppermute | solution.py:59
  131.8 88.3 %collective-permute-start.18 = (bf16[128,4096]{1,0:T(8,128)(2,1)S(1)}, bf16[128,4096]{1,0:T(8,128)(2,1)S(1)}, u32[]{:S(2)}, u32[]{:S(2)}) collective-permute-start(bf16[128,4096]{1,0:T(8,128)(2,1)S(1)} %copy-done.7), channel_id=1, source_target_pairs={{0,8},{2,10},{4,12},{6,14},{8,0},{10,2},{12,4},{14,6},{1,9},{3,11}... | collective-permute-start | bytes 3145736 | tf_op jit(solution)/shard_map/ppermute | solution.py:59
  135.4 89.8 %collective-permute-start.7 = (bf16[128,4224]{0,1:T(8,128)(2,1)}, bf16[128,4224]{0,1:T(8,128)(2,1)}, u32[]{:S(2)}, u32[]{:S(2)}) collective-permute-start(bf16[128,4224]{0,1:T(8,128)(2,1)} %collective-permute-done.2), channel_id=1, source_target_pairs={{0,2},{2,0},{4,6},{6,4},{8,10},{10,8},{12,14},{14,12},{1,3},{3,1},... | collective-permute-start | bytes 3244040 | tf_op jit(solution)/shard_map/ppermute | solution.py:62
  148.5 75.7 %collective-permute-start.19 = (bf16[128,4096]{1,0:T(8,128)(2,1)S(1)}, bf16[128,4096]{1,0:T(8,128)(2,1)S(1)}, u32[]{:S(2)}, u32[]{:S(2)}) collective-permute-start(bf16[128,4096]{1,0:T(8,128)(2,1)S(1)} %copy-done.7), channel_id=1, source_target_pairs={{0,12},{2,14},{4,0},{6,2},{8,4},{10,6},{12,8},{14,10},{1,13},{3,15... | collective-permute-start | bytes 3145736 | tf_op jit(solution)/shard_map/ppermute | solution.py:59
  150.1 161.5 %collective-permute-start.10 = (bf16[4096,384]{1,0:T(8,128)(2,1)}, bf16[4096,384]{1,0:T(8,128)(2,1)}, u32[]{:S(2)}, u32[]{:S(2)}) collective-permute-start(bf16[4096,384]{1,0:T(8,128)(2,1)} %dynamic-slice_bitcast_fusion), channel_id=1, source_target_pairs={{0,1},{1,0},{2,3},{3,2},{4,5},{5,4},{6,7},{7,6},{8,9},{9,8},{10,11... | collective-permute-start | bytes 9437192 | tf_op jit(solution)/shard_map/ppermute | solution.py:65
  200.4 113.6 %collective-permute-start.9 = (bf16[4096,384]{1,0:T(8,128)(2,1)}, bf16[4096,384]{1,0:T(8,128)(2,1)}, u32[]{:S(2)}, u32[]{:S(2)}) collective-permute-start(bf16[4096,384]{1,0:T(8,128)(2,1)} %collective-permute-done.8), channel_id=1, source_target_pairs={{0,16},{16,0},{1,17},{17,1},{2,18},{18,2},{3,19},{19,3},{4,20},{20... | collective-permute-start | bytes 9437192 | tf_op jit(solution)/shard_map/ppermute | solution.py:65
  220.2 97.8 %collective-permute-start.12 = (bf16[384,4096]{1,0:T(8,128)(2,1)}, bf16[384,4096]{1,0:T(8,128)(2,1)}, u32[]{:S(2)}, u32[]{:S(2)}) collective-permute-start(bf16[384,4096]{1,0:T(8,128)(2,1)} %collective-permute-done.6), channel_id=1, source_target_pairs={{0,16},{16,0},{1,17},{17,1},{2,18},{18,2},{3,19},{19,3},{4,20},{20... | collective-permute-start | bytes 9437192 | tf_op jit(solution)/shard_map/ppermute | solution.py:65
  255.8 47.1 %collective-permute-start.21 = (bf16[128,4096]{1,0:T(8,128)(2,1)}, bf16[128,4096]{1,0:T(8,128)(2,1)}, u32[]{:S(2)}, u32[]{:S(2)}) collective-permute-start(bf16[128,4096]{1,0:T(8,128)(2,1)} %collective-permute-done.17), channel_id=1, source_target_pairs={{0,2},{2,0},{4,6},{6,4},{8,10},{10,8},{12,14},{14,12},{1,3},{3,1},... | collective-permute-start | bytes 3145736 | tf_op jit(solution)/shard_map/ppermute | solution.py:62
  280.4 66.4 %collective-permute-start.22 = (bf16[128,4096]{1,0:T(8,128)(2,1)S(1)}, bf16[128,4096]{1,0:T(8,128)(2,1)S(1)}, u32[]{:S(2)}, u32[]{:S(2)}) collective-permute-start(bf16[128,4096]{1,0:T(8,128)(2,1)S(1)} %copy-done.9), channel_id=1, source_target_pairs={{0,2},{2,0},{4,6},{6,4},{8,10},{10,8},{12,14},{14,12},{1,3},{3,1},... | collective-permute-start | bytes 3145736 | tf_op jit(solution)/shard_map/ppermute | solution.py:62
  302.9 43.9 %collective-permute-start.23 = (bf16[128,4096]{1,0:T(8,128)(2,1)S(1)}, bf16[128,4096]{1,0:T(8,128)(2,1)S(1)}, u32[]{:S(2)}, u32[]{:S(2)}) collective-permute-start(bf16[128,4096]{1,0:T(8,128)(2,1)S(1)} %copy-done.11), channel_id=1, source_target_pairs={{0,2},{2,0},{4,6},{6,4},{8,10},{10,8},{12,14},{14,12},{1,3},{3,1},... | collective-permute-start | bytes 3145736 | tf_op jit(solution)/shard_map/ppermute | solution.py:62
  311.6 37.4 %collective-permute-start.11 = (bf16[4096,384]{1,0:T(8,128)(2,1)}, bf16[4096,384]{1,0:T(8,128)(2,1)S(1)}, u32[]{:S(2)}, u32[]{:S(2)}) collective-permute-start(bf16[4096,384]{1,0:T(8,128)(2,1)} %collective-permute-done.10), channel_id=1, source_target_pairs={{0,16},{16,0},{1,17},{17,1},{2,18},{18,2},{3,19},{19,3},{4,20},{20... | collective-permute-start | bytes 9437192 | tf_op jit(solution)/shard_map/ppermute | solution.py:65
  382.5 26.3 %collective-permute-start.13 = (bf16[128,4096]{1,0:T(8,128)(2,1)S(1)}, bf16[128,4096]{1,0:T(8,128)(2,1)}, u32[]{:S(2)}, u32[]{:S(2)}) collective-permute-start(bf16[128,4096]{1,0:T(8,128)(2,1)S(1)} %get-tuple-element.34), channel_id=1, source_target_pairs={{0,2},{2,0},{4,6},{6,4},{8,10},{10,8},{12,14},{14,12},{1,3},{3,1},... | collective-permute-start | bytes 3145736 | tf_op jit(solution)/shard_map/ppermute | solution.py:62
  384.0 45.3 %collective-permute-start.15 = (bf16[128,4096]{1,0:T(8,128)(2,1)}, bf16[128,4096]{1,0:T(8,128)(2,1)}, u32[]{:S(2)}, u32[]{:S(2)}) collective-permute-start(bf16[128,4096]{1,0:T(8,128)(2,1)} %get-tuple-element.36), channel_id=1, source_target_pairs={{0,2},{2,0},{4,6},{6,4},{8,10},{10,8},{12,14},{14,12},{1,3},{3,1},... | collective-permute-start | bytes 3145736 | tf_op jit(solution)/shard_map/ppermute | solution.py:62
  420.7 90.3 %collective-permute-start.14 = (bf16[128,4096]{1,0:T(8,128)(2,1)S(1)}, bf16[128,4096]{1,0:T(8,128)(2,1)}, u32[]{:S(2)}, u32[]{:S(2)}) collective-permute-start(bf16[128,4096]{1,0:T(8,128)(2,1)S(1)} %add_convert_fusion.3), channel_id=1, source_target_pairs={{0,8},{2,10},{4,12},{6,14},{8,0},{10,2},{12,4},{14,6},{1,9},{3,11}... | collective-permute-start | bytes 3145736 | tf_op jit(solution)/shard_map/ppermute | solution.py:59
  432.4 78.5 %collective-permute-start.16 = (bf16[128,4096]{1,0:T(8,128)(2,1)}, bf16[128,4096]{1,0:T(8,128)(2,1)}, u32[]{:S(2)}, u32[]{:S(2)}) collective-permute-start(bf16[128,4096]{1,0:T(8,128)(2,1)} %add_convert_fusion.2), channel_id=1, source_target_pairs={{0,12},{2,14},{4,0},{6,2},{8,4},{10,6},{12,8},{14,10},{1,13},{3,15... | collective-permute-start | bytes 3145736 | tf_op jit(solution)/shard_map/ppermute | solution.py:59
  444.6 26.2 %collective-permute-start.28 = (bf16[128,4096]{1,0:T(8,128)(2,1)S(1)}, bf16[128,4096]{1,0:T(8,128)(2,1)S(1)}, u32[]{:S(2)}, u32[]{:S(2)}) collective-permute-start(bf16[128,4096]{1,0:T(8,128)(2,1)S(1)} %get-tuple-element.47), channel_id=1, source_target_pairs={{0,2},{2,0},{4,6},{6,4},{8,10},{10,8},{12,14},{14,12},{1,3},{3,1},... | collective-permute-start | bytes 3145736 | tf_op jit(solution)/shard_map/ppermute | solution.py:62
  451.8 30.9 %collective-permute-start.30 = (bf16[128,4096]{1,0:T(8,128)(2,1)S(1)}, bf16[128,4096]{1,0:T(8,128)(2,1)S(1)}, u32[]{:S(2)}, u32[]{:S(2)}) collective-permute-start(bf16[128,4096]{1,0:T(8,128)(2,1)S(1)} %get-tuple-element.49), channel_id=1, source_target_pairs={{0,2},{2,0},{4,6},{6,4},{8,10},{10,8},{12,14},{14,12},{1,3},{3,1},... | collective-permute-start | bytes 3145736 | tf_op jit(solution)/shard_map/ppermute | solution.py:62
  471.0 40.0 %collective-permute-start.29 = (bf16[128,4096]{1,0:T(8,128)(2,1)S(1)}, bf16[128,4096]{1,0:T(8,128)(2,1)S(1)}, u32[]{:S(2)}, u32[]{:S(2)}) collective-permute-start(bf16[128,4096]{1,0:T(8,128)(2,1)S(1)} %add_convert_fusion.1), channel_id=1, source_target_pairs={{0,4},{2,6},{4,8},{6,10},{8,12},{10,14},{12,0},{14,2},{1,5},{3,7},... | collective-permute-start | bytes 3145736 | tf_op jit(solution)/shard_map/ppermute | solution.py:59
  (47 other events, 1166.9 us)

commit v5 on v4

--- a/solution.py
+++ b/solution.py
@@ -97,7 +97,7 @@
     marked, _ = lax.optimization_barrier((marked, sent[2]))
     token_blocks = spread(marked, {}, None, fetched[2])
     cotangent = follow(cotangent, (token_blocks[0], fetched[2]))
-    cot_blocks = spread(cotangent, {layers - 1: fetched[0]}, token_blocks[1][layers - 1])
+    cot_blocks = spread(cotangent, {layers - 1: fetched[0]}, token_blocks[1][layers - 2])
     cot_blocks[1][layers - 1] = follow(cot_blocks[1][layers - 1], fetched[1])
 
     def in_order(blocks, start, size):

time: 520 us -> 484 us (0.931)
  waiting for transfers between devices: 257 us -> 228 us
    ppermute x13, waiting for transfers between devices: 111 us -> 90.4 us  [swap(): lax.ppermute(block, 'expert', [(e, e ^ 1) for e in range(2 * layers)])]
    ppermute x12, waiting for transfers between devices: 133 us -> 125 us  [shift(): return lax.ppermute(block, 'expert', pairs)]
    unnamed x83 -> x85, local copies, waits for them, and re-layouts: 18.9 us -> 17.2 us
  transfers between devices with their start and end apart: 33 -> 33, of which waited for: 19 -> 17; matrix products, arithmetic and copies ran while one was open for 34% -> 35% of each run, Pallas kernels for 0% -> 0%
where the time goes in v5:
time: 484 us; the launch traced here: 478 us
  waiting for transfers between devices  228 us (47%)
  matrix products  105 us (22%)
  local copies, waits for them, and re-layouts  84.8 us (18%)
  starting transfers between devices  35.1 us (7%)
  other arithmetic  23.4 us (5%)
    ppermute x12, waiting for transfers between devices, shift(): return lax.ppermute(block, 'expert', pairs)  125 us
    ppermute x13, waiting for transfers between devices, swap(): lax.ppermute(block, 'expert', [(e, e ^ 1) for e in range(2 * layers)])  90.4 us
    dot_general x4, matrix products, expert_on(): jnp.dot(hidden, down_mat, preferred_element_type=jnp.float32)  60.5 us
    dot_general x3, matrix products, expert_on(): up_act = jnp.dot(rows_in, up_mat, preferred_element_type=jnp.float32)  21.7 us
    dynamic_update_slice x24, local copies, waits for them, and re-layouts, in_order(): lax.dynamic_update_slice(whole, block[:, start:start + size], (at, 0))  21 us
    slice x16, local copies, waits for them, and re-layouts, in_order(): block[:, start:start + size]  17.4 us
    unnamed x85, local copies, waits for them, and re-layouts  17.2 us
    ppermute x12, starting transfers between devices, shift(): return lax.ppermute(block, 'expert', pairs)  16.8 us
  transfers between devices with their start and end apart: 33, of which 17 were waited for; matrix products, arithmetic and copies ran while one was open for 35% of the time, Pallas kernels for 0%

profile of v5, /device:TPU:12, one launch (start us, length us, event | category | flops | bytes accessed | tf_op | source)
XLA Modules:
  0.0 478.1 jit_solution(11415004699206846151)
XLA Ops:
  30.3 6.6 %collective-permute-done.3 = bf16[128,4224]{0,1:T(8,128)(2,1)} collective-permute-done((bf16[128,4224]{0,1:T(8,128)(2,1)S(1)}, bf16[128,4224]{0,1:T(8,128)(2,1)}, u32[]{:S(2)}, u32[]{:S(2)}) %collective-permute-start.3) | collective-permute-done | bytes 1081376 | tf_op jit(solution)/shard_map/ppermute | solution.py:62
  40.2 39.1 %collective-permute-done = bf16[128,4224]{0,1:T(8,128)(2,1)} collective-permute-done((bf16[128,4224]{0,1:T(8,128)(2,1)S(1)}, bf16[128,4224]{0,1:T(8,128)(2,1)}, u32[]{:S(2)}, u32[]{:S(2)}) %collective-permute-start) | collective-permute-done | bytes 1081376 | tf_op jit(solution)/shard_map/ppermute | solution.py:59
  80.8 20.5 %collective-permute-done.1 = bf16[128,4224]{0,1:T(8,128)(2,1)} collective-permute-done((bf16[128,4224]{0,1:T(8,128)(2,1)S(1)}, bf16[128,4224]{0,1:T(8,128)(2,1)}, u32[]{:S(2)}, u32[]{:S(2)}) %collective-permute-start.1) | collective-permute-done | bytes 1081376 | tf_op jit(solution)/shard_map/ppermute | solution.py:59
  137.4 11.1 %collective-permute-done.8 = bf16[4096,384]{1,0:T(8,128)(2,1)} collective-permute-done((bf16[4096,384]{1,0:T(8,128)(2,1)}, bf16[4096,384]{1,0:T(8,128)(2,1)}, u32[]{:S(2)}, u32[]{:S(2)}) %collective-permute-start.8) | collective-permute-done | bytes 3145760 | tf_op jit(solution)/shard_map/ppermute | solution.py:65
  150.0 8.6 %fusion.13 = f32[512,768]{1,0:T(8,128)} fusion(bf16[512,4096]{1,0:T(8,128)(2,1)} %constant_dynamic-update-slice_fusion.22, bf16[1,4096,768]{2,1,0:T(8,128)(2,1)} %param.11), kind=kOutput, calls=%fused_computation.22 | convolution fusion | flops 3221225472 | bytes 12058624 | tf_op jit(solution)/shard_map/dot_general | solution.py:126
  158.6 17.1 %fusion.19 = bf16[512,4096]{1,0:T(8,128)(2,1)} fusion(bf16[1,768,4096]{2,1,0:T(8,128)(2,1)} %param.12, f32[512,768]{1,0:T(8,128)} %fusion.13, bf16[512,4096]{1,0:T(8,128)(2,1)} %constant_dynamic-update-slice_fusion.22, bf16[1,4096,768]{2,1,0:T(8,128)(2,1)} %param.10), kind=kOutput, calls=%fused_computation.28 | convolution fusion | flops 6446907392 | bytes 22544384 | tf_op jit(solution)/shard_map/dot_general | solution.py:128
  185.4 15.0 %collective-permute-done.17 = bf16[128,4096]{1,0:T(8,128)(2,1)} collective-permute-done((bf16[128,4096]{1,0:T(8,128)(2,1)S(1)}, bf16[128,4096]{1,0:T(8,128)(2,1)}, u32[]{:S(2)}, u32[]{:S(2)}) %collective-permute-start.17) | collective-permute-done | bytes 1048608 | tf_op jit(solution)/shard_map/ppermute | solution.py:59
  201.7 18.4 %collective-permute-done.18 = bf16[128,4096]{1,0:T(8,128)(2,1)} collective-permute-done((bf16[128,4096]{1,0:T(8,128)(2,1)S(1)}, bf16[128,4096]{1,0:T(8,128)(2,1)}, u32[]{:S(2)}, u32[]{:S(2)}) %collective-permute-start.18) | collective-permute-done | bytes 1048608 | tf_op jit(solution)/shard_map/ppermute | solution.py:59
  230.8 7.0 %fusion.11 = f32[512,768]{1,0:T(8,128)S(1)} fusion(bf16[512,4096]{1,0:T(8,128)(2,1)} %constant_dynamic-update-slice_fusion.18, bf16[1,4096,768]{2,1,0:T(8,128)(2,1)} %param.11), kind=kOutput, calls=%fused_computation.20 | convolution fusion | flops 3221225472 | bytes 12058624 | tf_op jit(solution)/shard_map/dot_general | solution.py:126
  238.5 16.6 %fusion.22 = bf16[512,4096]{1,0:T(8,128)(2,1)} fusion(bf16[1,768,4096]{2,1,0:T(8,128)(2,1)} %param.12, f32[512,768]{1,0:T(8,128)S(1)} %fusion.11, bf16[512,4096]{1,0:T(8,128)(2,1)} %constant_dynamic-update-slice_fusion.18, bf16[1,4096,768]{2,1,0:T(8,128)(2,1)} %param.10), kind=kOutput, calls=%fused_computation.29 | convolution fusion | flops 6446907392 | bytes 22544384 | tf_op jit(solution)/shard_map/dot_general | solution.py:128
  255.2 4.7 fusion.43
  259.9 8.0 %pad_maximum_fusion = bf16[1024,4096]{1,0:T(8,128)(2,1)} fusion(bf16[512,4096]{1,0:T(8,128)(2,1)} %constant_dynamic-update-slice_fusion.18, bf16[512,4096]{1,0:T(8,128)(2,1)} %constant_dynamic-update-slice_fusion.22), kind=kLoop, calls=%fused_computation.15 | loop fusion | flops 16777216 | bytes 16777216 | tf_op jit(solution)/shard_map/concatenate | solution.py:117
  273.9 20.6 %collective-permute-done.23 = bf16[128,4096]{1,0:T(8,128)(2,1)S(1)} collective-permute-done((bf16[128,4096]{1,0:T(8,128)(2,1)S(1)}, bf16[128,4096]{1,0:T(8,128)(2,1)S(1)}, u32[]{:S(2)}, u32[]{:S(2)}) %collective-permute-start.23) | collective-permute-done | bytes 1048608 | tf_op jit(solution)/shard_map/ppermute | solution.py:62
  305.4 7.2 %fusion.52 = f32[512,768]{1,0:T(8,128)S(1)} fusion(bf16[512,4096]{1,0:T(8,128)(2,1)} %constant_dynamic-update-slice_fusion.18, bf16[4096,768]{1,0:T(8,128)(2,1)S(1)} %constant_dynamic-update-slice_fusion), kind=kOutput, calls=%fused_computation.137 | convolution fusion | flops 3221225472 | bytes 12058624 | tf_op jit(solution)/shard_map/dot_general | solution.py:125
  316.0 19.0 %fusion.5 = (f32[512]{0:T(512)S(1)}, f32[512]{0:T(512)S(1)}, bf16[512,4096]{1,0:T(8,128)(2,1)}) fusion(bf16[512,4096]{1,0:T(8,128)(2,1)} %constant_dynamic-update-slice_fusion.10, bf16[512,4096]{1,0:T(8,128)(2,1)} %fusion.22, f32[512]{0:T(512)S(1)} %get-tuple-element.60, f32[512]{0:T(512)S(1)} %get-tuple-element.57, bf16[768,4096]{1,0:T(8,128)(2,1)} %copy-done.5, ...), kind=kOutput, calls=%fused_computation.13 | convolution fusion | flops 6469975040 | bytes 30941184 | tf_op jit(solution)/shard_map/dot_general | solution.py:128
  339.4 6.0 %fusion.53 = f32[512,768]{1,0:T(8,128)S(1)} fusion(bf16[512,4096]{1,0:T(8,128)(2,1)} %constant_dynamic-update-slice_fusion.22, bf16[4096,768]{1,0:T(8,128)(2,1)S(1)} %copy-done.7), kind=kOutput, calls=%fused_computation.138 | convolution fusion | flops 3221225472 | bytes 12058624 | tf_op jit(solution)/shard_map/dot_general | solution.py:125
  347.5 6.1 %multiply_convert_fusion = bf16[512,768]{1,0:T(8,128)(2,1)S(1)} fusion(f32[512,768]{1,0:T(8,128)S(1)} %fusion.53, bf16[512,4096]{1,0:T(8,128)(2,1)} %constant_dynamic-update-slice_fusion.22, bf16[4096,768]{1,0:T(8,128)(2,1)S(1)} %bitcast.89), kind=kOutput, calls=%fused_computation.39 | convolution fusion | flops 3223584768 | bytes 12845056 | tf_op jit(solution)/shard_map/dot_general | solution.py:126
  353.6 18.1 %collective-permute-done.13 = bf16[128,4096]{1,0:T(8,128)(2,1)} collective-permute-done((bf16[128,4096]{1,0:T(8,128)(2,1)S(1)}, bf16[128,4096]{1,0:T(8,128)(2,1)}, u32[]{:S(2)}, u32[]{:S(2)}) %collective-permute-start.13) | collective-permute-done | bytes 1048608 | tf_op jit(solution)/shard_map/ppermute | solution.py:62
  371.7 7.7 %fusion.3 = (f32[512]{0:T(512)S(1)}, f32[512]{0:T(512)S(1)}, f32[512,4096]{1,0:T(8,128)}) fusion(bf16[512,4096]{1,0:T(8,128)(2,1)S(1)} %copy-done.4, bf16[512,4096]{1,0:T(8,128)(2,1)S(1)} %copy-done.28, f32[512]{0:T(512)S(1)} %get-tuple-element.61, f32[512]{0:T(512)S(1)} %get-tuple-element.56, bf16[512,768]{1,0:T(8,128)(2,1)S(1)} %multiply_convert_fusion, ...), kind=kOutput, calls=%fused_computation.11 | convolution fusion | flops 3244293120 | bytes 23863296 | tf_op jit(solution)/shard_map/dot_general | solution.py:128
  386.8 5.6 %collective-permute-done.15 = bf16[128,4096]{1,0:T(8,128)(2,1)} collective-permute-done((bf16[128,4096]{1,0:T(8,128)(2,1)}, bf16[128,4096]{1,0:T(8,128)(2,1)}, u32[]{:S(2)}, u32[]{:S(2)}) %collective-permute-start.15) | collective-permute-done | bytes 1048608 | tf_op jit(solution)/shard_map/ppermute | solution.py:62
  401.9 5.1 %fusion.37 = f32[2,4096,48]{1,2,0:T(8,128)S(1)} fusion(bf16[2,512,4096]{2,1,0:T(8,128)(2,1)} %bitcast.79, bf16[6,2,8,512]{3,2,1,0:T(8,128)(2,1)S(1)} %bitcast.90), kind=kOutput, calls=%fused_computation.52 | convolution fusion | flops 402653184 | bytes 10059776 | tf_op jit(solution)/shard_map/dot_general | solution.py:174
  408.4 18.1 %collective-permute-done.28 = bf16[128,4096]{1,0:T(8,128)(2,1)S(1)} collective-permute-done((bf16[128,4096]{1,0:T(8,128)(2,1)S(1)}, bf16[128,4096]{1,0:T(8,128)(2,1)S(1)}, u32[]{:S(2)}, u32[]{:S(2)}) %collective-permute-start.28) | collective-permute-done | bytes 1048608 | tf_op jit(solution)/shard_map/ppermute | solution.py:62
  431.2 14.3 %collective-permute-done.30 = bf16[128,4096]{1,0:T(8,128)(2,1)S(1)} collective-permute-done((bf16[128,4096]{1,0:T(8,128)(2,1)S(1)}, bf16[128,4096]{1,0:T(8,128)(2,1)S(1)}, u32[]{:S(2)}, u32[]{:S(2)}) %collective-permute-start.30) | collective-permute-done | bytes 1048608 | tf_op jit(solution)/shard_map/ppermute | solution.py:62
  445.6 29.1 %collective-permute-done.16 = bf16[128,4096]{1,0:T(8,128)(2,1)} collective-permute-done((bf16[128,4096]{1,0:T(8,128)(2,1)}, bf16[128,4096]{1,0:T(8,128)(2,1)}, u32[]{:S(2)}, u32[]{:S(2)}) %collective-permute-start.16) | collective-permute-done | bytes 1048608 | tf_op jit(solution)/shard_map/ppermute | solution.py:59
  (232 shorter events, 146.6 us)
Async XLA Ops:
  7.1 72.2 %collective-permute-start = (bf16[128,4224]{0,1:T(8,128)(2,1)S(1)}, bf16[128,4224]{0,1:T(8,128)(2,1)}, u32[]{:S(2)}, u32[]{:S(2)}) collective-permute-start(bf16[128,4224]{0,1:T(8,128)(2,1)S(1)} %pad_maximum_fusion.1), channel_id=1, source_target_pairs={{0,4},{2,6},{4,8},{6,10},{8,12},{10,14},{12,0},{14,2},{1,5},{3,7},... | collective-permute-start | bytes 3244040 | tf_op jit(solution)/shard_map/ppermute | solution.py:59
  8.7 92.6 %collective-permute-start.1 = (bf16[128,4224]{0,1:T(8,128)(2,1)S(1)}, bf16[128,4224]{0,1:T(8,128)(2,1)}, u32[]{:S(2)}, u32[]{:S(2)}) collective-permute-start(bf16[128,4224]{0,1:T(8,128)(2,1)S(1)} %pad_maximum_fusion.1), channel_id=1, source_target_pairs={{0,8},{2,10},{4,12},{6,14},{8,0},{10,2},{12,4},{14,6},{1,9},{3,11}... | collective-permute-start | bytes 3244040 | tf_op jit(solution)/shard_map/ppermute | solution.py:59
  9.9 104.1 %collective-permute-start.2 = (bf16[128,4224]{0,1:T(8,128)(2,1)S(1)}, bf16[128,4224]{0,1:T(8,128)(2,1)}, u32[]{:S(2)}, u32[]{:S(2)}) collective-permute-start(bf16[128,4224]{0,1:T(8,128)(2,1)S(1)} %pad_maximum_fusion.1), channel_id=1, source_target_pairs={{0,12},{2,14},{4,0},{6,2},{8,4},{10,6},{12,8},{14,10},{1,13},{3,15... | collective-permute-start | bytes 3244040 | tf_op jit(solution)/shard_map/ppermute | solution.py:59
  11.8 120.1 %collective-permute-start.6 = (bf16[384,4096]{1,0:T(8,128)(2,1)}, bf16[384,4096]{1,0:T(8,128)(2,1)}, u32[]{:S(2)}, u32[]{:S(2)}) collective-permute-start(bf16[384,4096]{1,0:T(8,128)(2,1)} %dynamic-slice_bitcast_fusion.2), channel_id=1, source_target_pairs={{0,1},{1,0},{2,3},{3,2},{4,5},{5,4},{6,7},{7,6},{8,9},{9,8},{10,11... | collective-permute-start | bytes 9437192 | tf_op jit(solution)/shard_map/ppermute | solution.py:65
  36.8 111.6 %collective-permute-start.8 = (bf16[4096,384]{1,0:T(8,128)(2,1)}, bf16[4096,384]{1,0:T(8,128)(2,1)}, u32[]{:S(2)}, u32[]{:S(2)}) collective-permute-start(bf16[4096,384]{1,0:T(8,128)(2,1)} %dynamic-slice_bitcast_fusion.1), channel_id=1, source_target_pairs={{0,1},{1,0},{2,3},{3,2},{4,5},{5,4},{6,7},{7,6},{8,9},{9,8},{10,11... | collective-permute-start | bytes 9437192 | tf_op jit(solution)/shard_map/ppermute | solution.py:65
  79.3 42.3 %collective-permute-start.4 = (bf16[128,4224]{0,1:T(8,128)(2,1)}, bf16[128,4224]{0,1:T(8,128)(2,1)}, u32[]{:S(2)}, u32[]{:S(2)}) collective-permute-start(bf16[128,4224]{0,1:T(8,128)(2,1)} %collective-permute-done), channel_id=1, source_target_pairs={{0,2},{2,0},{4,6},{6,4},{8,10},{10,8},{12,14},{14,12},{1,3},{3,1},... | collective-permute-start | bytes 3244040 | tf_op jit(solution)/shard_map/ppermute | solution.py:62
  131.8 68.6 %collective-permute-start.17 = (bf16[128,4096]{1,0:T(8,128)(2,1)S(1)}, bf16[128,4096]{1,0:T(8,128)(2,1)}, u32[]{:S(2)}, u32[]{:S(2)}) collective-permute-start(bf16[128,4096]{1,0:T(8,128)(2,1)S(1)} %copy-done.9), channel_id=1, source_target_pairs={{0,4},{2,6},{4,8},{6,10},{8,12},{10,14},{12,0},{14,2},{1,5},{3,7},... | collective-permute-start | bytes 3145736 | tf_op jit(solution)/shard_map/ppermute | solution.py:59
  131.8 88.3 %collective-permute-start.18 = (bf16[128,4096]{1,0:T(8,128)(2,1)S(1)}, bf16[128,4096]{1,0:T(8,128)(2,1)}, u32[]{:S(2)}, u32[]{:S(2)}) collective-permute-start(bf16[128,4096]{1,0:T(8,128)(2,1)S(1)} %copy-done.9), channel_id=1, source_target_pairs={{0,8},{2,10},{4,12},{6,14},{8,0},{10,2},{12,4},{14,6},{1,9},{3,11}... | collective-permute-start | bytes 3145736 | tf_op jit(solution)/shard_map/ppermute | solution.py:59
  135.4 90.4 %collective-permute-start.7 = (bf16[128,4224]{0,1:T(8,128)(2,1)}, bf16[128,4224]{0,1:T(8,128)(2,1)}, u32[]{:S(2)}, u32[]{:S(2)}) collective-permute-start(bf16[128,4224]{0,1:T(8,128)(2,1)} %collective-permute-done.2), channel_id=1, source_target_pairs={{0,2},{2,0},{4,6},{6,4},{8,10},{10,8},{12,14},{14,12},{1,3},{3,1},... | collective-permute-start | bytes 3244040 | tf_op jit(solution)/shard_map/ppermute | solution.py:62
  136.9 47.3 %collective-permute-start.20 = (bf16[128,4096]{1,0:T(8,128)(2,1)S(1)}, bf16[128,4096]{1,0:T(8,128)(2,1)S(1)}, u32[]{:S(2)}, u32[]{:S(2)}) collective-permute-start(bf16[128,4096]{1,0:T(8,128)(2,1)S(1)} %copy-done.9), channel_id=1, source_target_pairs={{0,2},{2,0},{4,6},{6,4},{8,10},{10,8},{12,14},{14,12},{1,3},{3,1},... | collective-permute-start | bytes 3145736 | tf_op jit(solution)/shard_map/ppermute | solution.py:62
  148.5 75.6 %collective-permute-start.19 = (bf16[128,4096]{1,0:T(8,128)(2,1)S(1)}, bf16[128,4096]{1,0:T(8,128)(2,1)S(1)}, u32[]{:S(2)}, u32[]{:S(2)}) collective-permute-start(bf16[128,4096]{1,0:T(8,128)(2,1)S(1)} %copy-done.9), channel_id=1, source_target_pairs={{0,12},{2,14},{4,0},{6,2},{8,4},{10,6},{12,8},{14,10},{1,13},{3,15... | collective-permute-start | bytes 3145736 | tf_op jit(solution)/shard_map/ppermute | solution.py:59
  184.2 86.8 %collective-permute-start.10 = (bf16[4096,384]{1,0:T(8,128)(2,1)}, bf16[4096,384]{1,0:T(8,128)(2,1)}, u32[]{:S(2)}, u32[]{:S(2)}) collective-permute-start(bf16[4096,384]{1,0:T(8,128)(2,1)} %dynamic-slice_bitcast_fusion), channel_id=1, source_target_pairs={{0,1},{1,0},{2,3},{3,2},{4,5},{5,4},{6,7},{7,6},{8,9},{9,8},{10,11... | collective-permute-start | bytes 9437192 | tf_op jit(solution)/shard_map/ppermute | solution.py:65
  200.4 97.9 %collective-permute-start.9 = (bf16[4096,384]{1,0:T(8,128)(2,1)}, bf16[4096,384]{1,0:T(8,128)(2,1)}, u32[]{:S(2)}, u32[]{:S(2)}) collective-permute-start(bf16[4096,384]{1,0:T(8,128)(2,1)} %collective-permute-done.8), channel_id=1, source_target_pairs={{0,16},{16,0},{1,17},{17,1},{2,18},{18,2},{3,19},{19,3},{4,20},{20... | collective-permute-start | bytes 9437192 | tf_op jit(solution)/shard_map/ppermute | solution.py:65
  220.2 80.7 %collective-permute-start.12 = (bf16[384,4096]{1,0:T(8,128)(2,1)}, bf16[384,4096]{1,0:T(8,128)(2,1)}, u32[]{:S(2)}, u32[]{:S(2)}) collective-permute-start(bf16[384,4096]{1,0:T(8,128)(2,1)} %collective-permute-done.6), channel_id=1, source_target_pairs={{0,16},{16,0},{1,17},{17,1},{2,18},{18,2},{3,19},{19,3},{4,20},{20... | collective-permute-start | bytes 9437192 | tf_op jit(solution)/shard_map/ppermute | solution.py:65
  224.1 43.8 %collective-permute-start.21 = (bf16[128,4096]{1,0:T(8,128)(2,1)}, bf16[128,4096]{1,0:T(8,128)(2,1)}, u32[]{:S(2)}, u32[]{:S(2)}) collective-permute-start(bf16[128,4096]{1,0:T(8,128)(2,1)} %collective-permute-done.17), channel_id=1, source_target_pairs={{0,2},{2,0},{4,6},{6,4},{8,10},{10,8},{12,14},{14,12},{1,3},{3,1},... | collective-permute-start | bytes 3145736 | tf_op jit(solution)/shard_map/ppermute | solution.py:62
  225.7 47.1 %collective-permute-start.22 = (bf16[128,4096]{1,0:T(8,128)(2,1)}, bf16[128,4096]{1,0:T(8,128)(2,1)S(1)}, u32[]{:S(2)}, u32[]{:S(2)}) collective-permute-start(bf16[128,4096]{1,0:T(8,128)(2,1)} %collective-permute-done.18), channel_id=1, source_target_pairs={{0,2},{2,0},{4,6},{6,4},{8,10},{10,8},{12,14},{14,12},{1,3},{3,1},... | collective-permute-start | bytes 3145736 | tf_op jit(solution)/shard_map/ppermute | solution.py:62
  267.9 26.6 %collective-permute-start.23 = (bf16[128,4096]{1,0:T(8,128)(2,1)S(1)}, bf16[128,4096]{1,0:T(8,128)(2,1)S(1)}, u32[]{:S(2)}, u32[]{:S(2)}) collective-permute-start(bf16[128,4096]{1,0:T(8,128)(2,1)S(1)} %copy-done.11), channel_id=1, source_target_pairs={{0,2},{2,0},{4,6},{6,4},{8,10},{10,8},{12,14},{14,12},{1,3},{3,1},... | collective-permute-start | bytes 3145736 | tf_op jit(solution)/shard_map/ppermute | solution.py:62
  271.0 41.6 %collective-permute-start.11 = (bf16[4096,384]{1,0:T(8,128)(2,1)}, bf16[4096,384]{1,0:T(8,128)(2,1)S(1)}, u32[]{:S(2)}, u32[]{:S(2)}) collective-permute-start(bf16[4096,384]{1,0:T(8,128)(2,1)} %collective-permute-done.10), channel_id=1, source_target_pairs={{0,16},{16,0},{1,17},{17,1},{2,18},{18,2},{3,19},{19,3},{4,20},{20... | collective-permute-start | bytes 9437192 | tf_op jit(solution)/shard_map/ppermute | solution.py:65
  345.4 26.3 %collective-permute-start.13 = (bf16[128,4096]{1,0:T(8,128)(2,1)S(1)}, bf16[128,4096]{1,0:T(8,128)(2,1)}, u32[]{:S(2)}, u32[]{:S(2)}) collective-permute-start(bf16[128,4096]{1,0:T(8,128)(2,1)S(1)} %get-tuple-element.34), channel_id=1, source_target_pairs={{0,2},{2,0},{4,6},{6,4},{8,10},{10,8},{12,14},{14,12},{1,3},{3,1},... | collective-permute-start | bytes 3145736 | tf_op jit(solution)/shard_map/ppermute | solution.py:62
  347.0 45.4 %collective-permute-start.15 = (bf16[128,4096]{1,0:T(8,128)(2,1)}, bf16[128,4096]{1,0:T(8,128)(2,1)}, u32[]{:S(2)}, u32[]{:S(2)}) collective-permute-start(bf16[128,4096]{1,0:T(8,128)(2,1)} %get-tuple-element.36), channel_id=1, source_target_pairs={{0,2},{2,0},{4,6},{6,4},{8,10},{10,8},{12,14},{14,12},{1,3},{3,1},... | collective-permute-start | bytes 3145736 | tf_op jit(solution)/shard_map/ppermute | solution.py:62
  385.1 89.5 %collective-permute-start.14 = (bf16[128,4096]{1,0:T(8,128)(2,1)S(1)}, bf16[128,4096]{1,0:T(8,128)(2,1)}, u32[]{:S(2)}, u32[]{:S(2)}) collective-permute-start(bf16[128,4096]{1,0:T(8,128)(2,1)S(1)} %add_convert_fusion.3), channel_id=1, source_target_pairs={{0,8},{2,10},{4,12},{6,14},{8,0},{10,2},{12,4},{14,6},{1,9},{3,11}... | collective-permute-start | bytes 3145736 | tf_op jit(solution)/shard_map/ppermute | solution.py:59
  395.5 79.1 %collective-permute-start.16 = (bf16[128,4096]{1,0:T(8,128)(2,1)}, bf16[128,4096]{1,0:T(8,128)(2,1)}, u32[]{:S(2)}, u32[]{:S(2)}) collective-permute-start(bf16[128,4096]{1,0:T(8,128)(2,1)} %add_convert_fusion.2), channel_id=1, source_target_pairs={{0,12},{2,14},{4,0},{6,2},{8,4},{10,6},{12,8},{14,10},{1,13},{3,15... | collective-permute-start | bytes 3145736 | tf_op jit(solution)/shard_map/ppermute | solution.py:59
  407.7 37.9 %collective-permute-start.30 = (bf16[128,4096]{1,0:T(8,128)(2,1)S(1)}, bf16[128,4096]{1,0:T(8,128)(2,1)S(1)}, u32[]{:S(2)}, u32[]{:S(2)}) collective-permute-start(bf16[128,4096]{1,0:T(8,128)(2,1)S(1)} %get-tuple-element.49), channel_id=1, source_target_pairs={{0,2},{2,0},{4,6},{6,4},{8,10},{10,8},{12,14},{14,12},{1,3},{3,1},... | collective-permute-start | bytes 3145736 | tf_op jit(solution)/shard_map/ppermute | solution.py:62
  426.8 47.9 %collective-permute-start.29 = (bf16[128,4096]{1,0:T(8,128)(2,1)S(1)}, bf16[128,4096]{1,0:T(8,128)(2,1)S(1)}, u32[]{:S(2)}, u32[]{:S(2)}) collective-permute-start(bf16[128,4096]{1,0:T(8,128)(2,1)S(1)} %add_convert_fusion.1), channel_id=1, source_target_pairs={{0,4},{2,6},{4,8},{6,10},{8,12},{10,14},{12,0},{14,2},{1,5},{3,7},... | collective-permute-start | bytes 3145736 | tf_op jit(solution)/shard_map/ppermute | solution.py:59
  (48 other events, 1064.2 us)
